TPU v7x, 512 devices: a whole 4x8x8 slice. The times are simulated.
512 devices in a mesh: wide: 128 (over y, x, z_lo), narrow: 4 (over z_hi, core).
Axes of the slice: x: 4, y: 8, z: 8 (z_hi: 2, z_lo: 4; z = z_hi * 4 + z_lo), core: 2. Of those that a mesh axis runs over, the one named last changes fastest.
Arguments:
- state_rhs: float32 [3, 1024, 128, 256], P(None, 'wide', 'narrow'), may hold values from -8 to 8
- adjoint_rhs: float32 [3, 1024, 128, 256], P(None, 'wide', 'narrow'), may hold values from -8 to 8
- penalty: float32 [1024, 128, 256], P('wide', 'narrow'), may hold values from 0.05 to 20
- margin_width: int32 [128, 4], P('wide', 'narrow'), may hold values from 1 to 3
- owner_map: int32 [128, 4], replicated, may hold values from 0 to 63
- coarse_inv: float32 [64, 64], replicated, may hold values from -1 to 1
Outputs:
- state_update: float32 [3, 1024, 128, 256], P(None, 'wide', 'narrow')
- adjoint_update: float32 [3, 1024, 128, 256], P(None, 'wide', 'narrow')
- sensitivity: float32 [1024, 128, 256], P('wide', 'narrow')
All inputs are finite; a program needn't handle non-finite values. Where the computation divides by a largest or mean magnitude, that divisor is 1e-20 or more.
Results may differ from a plain program's by a relative error of at most 0.00018.
Values sent between devices are 32-bit elements; how exact they have to be, the bound alone decides.
A program may use at most 64 MiB of HBM per device.

v0:
```python
import jax
import jax.numpy as jnp
from jax import lax
from jax.sharding import PartitionSpec as P

OV = 3
SWEEPS = 4


GRAD_DIV_WEIGHT = 1.0
DAMPING = 0.7
PEAK_EPS = 1e-06


def extended_2(block, sides, width, periodic):
    for axis, dim in sides:
        count = lax.axis_size(axis)
        forward = [(i, i + 1) for i in range(count - 1)]
        if periodic:
            forward.append((count - 1, 0))
        backward = [(target, source) for source, target in forward]
        low = lax.ppermute(
            lax.slice_in_dim(block, block.shape[dim] - width, None, axis=dim), axis, forward
        )
        high = lax.ppermute(lax.slice_in_dim(block, 0, width, axis=dim), axis, backward)
        block = jnp.concatenate([low, block, high], axis=dim)
    return block


def passed_along(block, axis, distance):
    devices = range(lax.axis_size(axis))
    route = [((i - distance) % len(devices), i) for i in devices]
    return lax.ppermute(block, axis, route)


def passed_along_2(value, axis, steps):
    count = lax.axis_size(axis)
    initial, last = (max(0, -steps), min(count, count - steps))
    return lax.ppermute(value, axis, [(source, source + steps) for source in range(initial, last)])


def apply_operator(iterate, penalty_box):
    padded = jnp.pad(iterate, ((0, 0), (1, 1), (1, 1), (1, 1)))
    ext_a, ext_b, ext_c = (iterate.shape[1], iterate.shape[2], iterate.shape[3])

    def shifted(c, step):
        return padded[
            c,
            1 + step[0] : 1 + step[0] + ext_a,
            1 + step[1] : 1 + step[1] + ext_b,
            1 + step[2] : 1 + step[2] + ext_c,
        ]

    unit_steps = ((1, 0, 0), (0, 1, 0), (0, 0, 1))
    result_rows = []
    for c in range(3):
        centre = iterate[c]
        beside = jnp.zeros_like(centre)
        for unit in unit_steps:
            beside = beside + shifted(c, unit) + shifted(c, tuple((-v for v in unit)))
        own_unit = unit_steps[c]
        grad_div = shifted(c, own_unit) + shifted(c, tuple((-v for v in own_unit))) - 2.0 * centre
        for d in range(3):
            if d != c:
                other = unit_steps[d]
                plus_plus = tuple((own_unit[t] + other[t] for t in range(3)))
                plus_minus = tuple((own_unit[t] - other[t] for t in range(3)))
                grad_div = grad_div + 0.25 * (
                    shifted(d, plus_plus)
                    - shifted(d, plus_minus)
                    - shifted(d, tuple((-v for v in plus_minus)))
                    + shifted(d, tuple((-v for v in plus_plus)))
                )
        result_rows.append(
            6.0 * centre - beside + penalty_box * centre - GRAD_DIV_WEIGHT * grad_div
        )
    return jnp.stack(result_rows, 0)


def local_solve(source, penalty_box, inside):
    diagonal = 6.0 + penalty_box + 2.0 * GRAD_DIV_WEIGHT
    iterate = jnp.zeros_like(source)
    for iteration in range(SWEEPS):
        iterate = inside * (
            iterate + DAMPING * (source - apply_operator(iterate, penalty_box)) / diagonal
        )
    return iterate


def fold_along(values, dim, inner, sender):
    extent = values.shape[dim]
    lower_rim = lax.slice_in_dim(values, 0, OV, axis=dim)
    upper_rim = lax.slice_in_dim(values, extent - OV, extent, axis=dim)
    for stride, rim_part, start in ((-1, lower_rim, inner), (1, upper_rim, OV)):
        arrived = sender(rim_part, stride)
        current = lax.slice_in_dim(values, start, start + OV, axis=dim)
        values = lax.dynamic_update_slice_in_dim(values, current + arrived, start, dim)
    return lax.slice_in_dim(values, OV, OV + inner, axis=dim)


def body(state_rhs, adjoint_rhs, penalty, margin_width, owner_map, coarse_inv):
    width_x, width_y = (state_rhs.shape[1], state_rhs.shape[2])
    packed = jnp.concatenate([state_rhs, penalty[None]], 0)
    widened = extended_2(packed, (("wide", 1),), OV, True)
    extended = extended_2(widened, (("narrow", 2),), OV, False)
    source = extended[:3]
    penalty_box = extended[3]
    reach_cells = margin_width[0, 0]
    row_x = jnp.arange(width_x + 2 * OV, dtype=jnp.int32) - OV
    row_y = jnp.arange(width_y + 2 * OV, dtype=jnp.int32) - OV
    global_y = lax.axis_index("narrow") * width_y + row_y
    in_x = (row_x >= -reach_cells) & (row_x < width_x + reach_cells)
    in_y = (
        (row_y >= -reach_cells)
        & (row_y < width_y + reach_cells)
        & (global_y >= 0)
        & (global_y < width_y * lax.axis_size("narrow"))
    )
    inside = (in_x[:, None] & in_y[None, :]).astype(jnp.float32)[:, :, None]
    solved = local_solve(inside * source, penalty_box, inside)
    state_local = solved[:, OV : OV + width_x, OV : OV + width_y]
    adj_source = jnp.pad(adjoint_rhs, ((0, 0), (OV, OV), (OV, OV), (0, 0)))
    adj_solved = local_solve(inside * adj_source, penalty_box, inside)
    folded = fold_along(
        adj_solved, 1, width_x, lambda rim_part, stride: passed_along(rim_part, "wide", stride)
    )
    adjoint_local = fold_along(
        folded, 2, width_y, lambda rim_part, stride: passed_along_2(rim_part, "narrow", stride)
    )
    groups = coarse_inv.shape[0]
    highest = lax.Precision.HIGHEST
    block_means = jnp.concatenate(
        [jnp.mean(state_rhs, axis=(1, 2, 3)), jnp.mean(adjoint_rhs, axis=(1, 2, 3))], 0
    )
    owner_flat = owner_map.reshape(-1)
    my_slot = lax.axis_index("wide") * lax.axis_size("narrow") + lax.axis_index("narrow")
    own_group = jnp.sum(
        jnp.where(jnp.arange(owner_flat.shape[0], dtype=jnp.int32) == my_slot, owner_flat, 0)
    )
    my_pick = (jnp.arange(groups, dtype=jnp.int32) == own_group).astype(jnp.float32)
    coarse_rhs = lax.psum(block_means[:, None] * my_pick[None, :], ("wide", "narrow"))
    state_coarse = jnp.dot(coarse_rhs[:3], coarse_inv.T, precision=highest)
    state_corr = jnp.dot(state_coarse, my_pick, precision=highest) - jnp.mean(state_coarse, axis=1)
    centred = coarse_rhs[3:] - jnp.mean(coarse_rhs[3:], axis=1, keepdims=True)
    adjoint_coarse = jnp.dot(centred, coarse_inv, precision=highest)
    adj_corr = jnp.dot(adjoint_coarse, my_pick, precision=highest)
    state_update = state_local + state_corr[:, None, None, None]
    adjoint_update = adjoint_local + adj_corr[:, None, None, None]
    sens_raw = -jnp.sum(state_update * adjoint_update, axis=0)
    largest = lax.pmax(jnp.max(jnp.abs(sens_raw)), ("wide", "narrow"))
    sensitivity = sens_raw / (largest + PEAK_EPS)
    return (state_update, adjoint_update, sensitivity)


def solution(mesh):
    placed = (
        P(None, "wide", "narrow", None),
        P(None, "wide", "narrow", None),
        P("wide", "narrow", None),
        P("wide", "narrow"),
        P(),
        P(),
    )
    return jax.shard_map(
        body,
        mesh=mesh,
        in_specs=placed,
        out_specs=(
            P(None, "wide", "narrow", None),
            P(None, "wide", "narrow", None),
            P("wide", "narrow", None),
        ),
        check_vma=False,
    )
```

profile of v0, /device:TPU:1, one launch (start us, length us, event | category | flops | bytes accessed | tf_op | source)
XLA Modules:
  0.0 346.0 jit_solution(8652203681744874501)
XLA Ops:
  0.7 2.1 pad_maximum_fusion.4
  2.8 4.8 %collective-permute-start = (f32[4,3,32,256]{3,2,1,0:T(8,128)}, f32[4,3,32,256]{3,2,1,0:T(8,128)S(1)}, u32[]{:S(2)}, u32[]{:S(2)}) collective-permute-start(f32[4,3,32,256]{3,2,1,0:T(8,128)} %get-tuple-element.37), channel_id=1, source_target_pairs={{0,4},{4,8},{8,12},{12,16},{16,20},{20,24},{24,28},{28,32},{32,36}... | collective-permute-start | bytes 1179656 | tf_op jit(solution)/shard_map/ppermute | solution.py:22
  7.6 10.6 %collective-permute-start.1 = (f32[4,3,32,256]{3,2,1,0:T(8,128)S(1)}, f32[4,3,32,256]{3,2,1,0:T(8,128)S(1)}, u32[]{:S(2)}, u32[]{:S(2)}) collective-permute-start(f32[4,3,32,256]{3,2,1,0:T(8,128)S(1)} %get-tuple-element.38), channel_id=1, source_target_pairs={{4,0},{8,4},{12,8},{16,12},{20,16},{24,20},{28,24},{32,28},{36,32}... | collective-permute-start | bytes 1179656 | tf_op jit(solution)/shard_map/ppermute | solution.py:25
  18.3 0.6 select_reduce_fusion
  18.9 0.6 fusion.405
  19.6 0.2 reduce_sum.54
  19.7 0.2 reduce_sum.55
  19.9 0.1 pad_maximum_fusion.9
  20.7 101.5 %psum.7 = f32[6,64]{1,0:T(8,128)S(1)} all-reduce(f32[6,64]{1,0:T(8,128)S(1)} %broadcast_multiply_fusion), channel_id=1, replica_groups=mesh['wide'=128,'narrow'=4] {'wide','narrow'}, use_global_device_ids=true, to_apply=%region_3.4 | all-reduce | flops 384 | bytes 3072 | tf_op jit(solution)/shard_map/psum | solution.py:141
  122.3 0.1 slice_reduce_fusion
  122.4 0.1 pad_maximum_fusion.8
  122.5 6.4 %collective-permute-start.2 = (f32[4,14,3,256]{3,2,1,0:T(4,128)S(1)}, f32[4,14,3,256]{3,2,1,0:T(4,128)S(1)}, u32[]{:S(2)}, u32[]{:S(2)}) collective-permute-start(f32[4,14,3,256]{3,2,1,0:T(4,128)S(1)} %get-tuple-element.29), channel_id=1, source_target_pairs={{0,1},{1,2},{2,3},{4,5},{5,6},{6,7},{8,9},{9,10},{10,11},{12,13},{... | collective-permute-start | bytes 516104 | tf_op jit(solution)/shard_map/ppermute | solution.py:22
  129.0 1.9 collective-permute-start.3
  131.0 0.9 collective-permute-done.2
  131.9 8.9 %collective-permute-done.3 = f32[4,14,3,256]{3,2,1,0:T(4,128)S(1)} collective-permute-done((f32[4,14,3,256]{3,2,1,0:T(4,128)S(1)}, f32[4,14,3,256]{3,2,1,0:T(4,128)S(1)}, u32[]{:S(2)}, u32[]{:S(2)}) %collective-permute-start.3) | collective-permute-done | bytes 172064 | tf_op jit(solution)/shard_map/ppermute | solution.py:25
  140.8 0.1 add_bitcast_fusion
  141.0 2.8 fusion.54
  143.8 0.9 fusion.62
  144.7 0.3 pad_maximum_fusion
  145.1 0.4 copy-done.10
  145.5 2.5 slice_multiply_fusion
  148.0 21.3 %fusion.78 = (f32[1,14,38,256]{3,2,1,0:T(8,128)}, f32[1,14,38,256]{3,2,1,0:T(8,128)}, f32[1,14,38,256]{3,2,1,0:T(8,128)}, f32[1,14,38,256]{3,2,1,0:T(8,128)}, f3...) fusion(f32[3,14,38,256]{3,2,1,0:T(8,128)S(1)} %get-tuple-element.9, f32[1,14,38,256]{3,2,1,0:T(8,128)S(1)} %get-tuple-element.7, ...), kind=kLoop, calls=%fused_computation.366 | loop fusion | flops 18522112 | bytes 10723328 | tf_op jit(solution)/shard_map/sub | solution.py:75
  169.4 4.3 %fusion.3 = (f32[3,14,38,256]{3,2,1,0:T(8,128)S(1)}, f32[3,14,38,256]{3,2,1,0:T(8,128)S(1)}) fusion(f32[3,14,38,256]{3,2,1,0:T(8,128)} %copy-done.1, f32[1,14,38,256]{3,2,1,0:T(8,128)} %get-tuple-element.18, f32[1,14,38,256]{3,2,1,0:T(8,128)} %get-tuple-element.19, f32[1,14,38,256]{3,2,1,0:T(8,128)} %get-tuple-element.17, f32[14,38,256]{2,1,0:T(8,128)} %copy-done.6, ...), kind=kLoop, calls=%fused_computation.277 | loop fusion | flops 8988672 | bytes 12773456 | tf_op jit(solution)/shard_map/mul | solution.py:84
  173.7 4.2 %fusion.294 = (f32[1,14,38,256]{3,2,1,0:T(8,128)S(1)}, f32[1,14,38,256]{3,2,1,0:T(8,128)S(1)}, f32[1,14,38,256]{3,2,1,0:T(8,128)S(1)}) fusion(f32[3,14,38,256]{3,2,1,0:T(8,128)S(1)} %get-tuple-element.42, f32[1,14,38,256]{3,2,1,0:T(8,128)S(1)} %get-tuple-element.7), kind=kLoop, calls=%fused_computation.582 | loop fusion | flops 9261056 | bytes 5648384 | tf_op jit(solution)/shard_map/sub | solution.py:75
  177.9 1.7 fusion.15
  179.7 20.9 %fusion.132 = (f32[1,14,38,256]{3,2,1,0:T(8,128)}, f32[1,14,38,256]{3,2,1,0:T(8,128)}, f32[1,14,38,256]{3,2,1,0:T(8,128)}, f32[1,14,38,256]{3,2,1,0:T(8,128)}, f...) fusion(f32[3,14,38,256]{3,2,1,0:T(8,128)S(1)} %get-tuple-element.41, f32[1,14,38,256]{3,2,1,0:T(8,128)S(1)} %get-tuple-element.7, ...), kind=kLoop, calls=%fused_computation.420 | loop fusion | flops 18522112 | bytes 10723328 | tf_op jit(solution)/shard_map/sub | solution.py:75
  200.6 3.7 %fusion.7 = (f32[3,14,38,256]{3,2,1,0:T(8,128)S(1)}, f32[3,14,38,256]{3,2,1,0:T(8,128)S(1)}) fusion(f32[3,14,38,256]{3,2,1,0:T(8,128)S(1)} %get-tuple-element.41, f32[1,14,38,256]{3,2,1,0:T(8,128)} %get-tuple-element.15, f32[1,14,38,256]{3,2,1,0:T(8,128)} %get-tuple-element.16, f32[1,14,38,256]{3,2,1,0:T(8,128)} %get-tuple-element.14, ...), kind=kLoop, calls=%fused_computation.282 | loop fusion | flops 6537216 | bytes 12773456 | tf_op jit(solution)/shard_map/mul | solution.py:84
  204.3 6.2 %collective-permute-start.4 = (f32[3,3,38,256]{3,2,1,0:T(8,128)S(1)}, f32[3,3,38,256]{3,2,1,0:T(8,128)S(1)}, u32[]{:S(2)}, u32[]{:S(2)}) collective-permute-start(f32[3,3,38,256]{3,2,1,0:T(8,128)S(1)} %slice.1414), channel_id=1, source_target_pairs={{4,0},{8,4},{12,8},{16,12},{20,16},{24,20},{28,24},{32,28},{36,32}... | collective-permute-start | bytes 1050632 | tf_op jit(solution)/shard_map/ppermute | solution.py:33
  210.6 0.2 fusion.397
  210.8 4.3 %collective-permute-done.4 = f32[3,3,38,256]{3,2,1,0:T(8,128)S(1)} collective-permute-done((f32[3,3,38,256]{3,2,1,0:T(8,128)S(1)}, f32[3,3,38,256]{3,2,1,0:T(8,128)S(1)}, u32[]{:S(2)}, u32[]{:S(2)}) %collective-permute-start.4) | collective-permute-done | bytes 350240 | tf_op jit(solution)/shard_map/ppermute | solution.py:33
  215.0 0.1 fusion.409
  215.1 2.1 collective-permute-start.5
  217.2 0.3 fusion.410
  217.6 0.8 convolution_bitcast_fusion
  218.4 0.8 fusion.20
  219.1 11.0 %collective-permute-done.5 = f32[3,3,38,256]{3,2,1,0:T(8,128)S(1)} collective-permute-done((f32[3,3,38,256]{3,2,1,0:T(8,128)S(1)}, f32[3,3,38,256]{3,2,1,0:T(8,128)S(1)}, u32[]{:S(2)}, u32[]{:S(2)}) %collective-permute-start.5) | collective-permute-done | bytes 350240 | tf_op jit(solution)/shard_map/ppermute | solution.py:33
  230.1 0.1 fusion.395
  230.3 1.9 collective-permute-start.6
  232.2 4.2 %fusion.186 = (f32[1,14,38,256]{3,2,1,0:T(8,128)S(1)}, f32[1,14,38,256]{3,2,1,0:T(8,128)S(1)}, f32[1,14,38,256]{3,2,1,0:T(8,128)S(1)}) fusion(f32[3,14,38,256]{3,2,1,0:T(8,128)S(1)} %get-tuple-element.39, f32[1,14,38,256]{3,2,1,0:T(8,128)S(1)} %get-tuple-element.7), kind=kLoop, calls=%fused_computation.474 | loop fusion | flops 9261056 | bytes 5648384 | tf_op jit(solution)/shard_map/sub | solution.py:75
  236.5 1.0 slice.1401
  237.5 7.5 %collective-permute-start.7 = (f32[3,8,3,256]{3,2,1,0:T(4,128)S(1)}, f32[3,8,3,256]{3,2,1,0:T(4,128)S(1)}, u32[]{:S(2)}, u32[]{:S(2)}) collective-permute-start(f32[3,8,3,256]{3,2,1,0:T(4,128)S(1)} %get-tuple-element.31), channel_id=1, source_target_pairs={{0,1},{1,2},{2,3},{4,5},{5,6},{6,7},{8,9},{9,10},{10,11},{12,13},{... | collective-permute-start | bytes 221192 | tf_op jit(solution)/shard_map/ppermute | solution.py:39
  245.1 0.3 dynamic_update_slice.14
  245.4 1.3 collective-permute-done.7
  246.8 0.3 dynamic_update_slice.15
  247.1 3.3 multiply_reduce_fusion
  250.4 0.6 abs_reduce_fusion
  251.0 93.6 %pmax.7 = f32[]{:T(128)} all-reduce(f32[]{:T(128)} %abs_reduce_fusion), channel_id=1, replica_groups=mesh['wide'=128,'narrow'=4] {'wide','narrow'}, use_global_device_ids=true, to_apply=%region_8.9 | all-reduce | flops 1 | bytes 8 | tf_op jit(solution)/shard_map/pmax | solution.py:150
  345.3 0.7 negate_divide_fusion
  (42 shorter events, 0.5 us)
Async XLA Ops:
  0.6 209.9 %copy-start = (f32[64,64]{1,0:T(8,128)S(1)}, f32[64,64]{1,0:T(8,128)}, u32[]{:S(2)}) copy-start(f32[64,64]{1,0:T(8,128)} %param.11) | copy-start | bytes 49156
  0.6 18.9 %copy-start.5 = (f32[3,8,32,256]{3,2,1,0:T(8,128)S(1)}, f32[3,8,32,256]{3,2,1,0:T(8,128)}, u32[]{:S(2)}) copy-start(f32[3,8,32,256]{3,2,1,0:T(8,128)} %param.6) | copy-start | bytes 2359300
  0.7 17.6 %copy-start.12 = (s32[128,4]{0,1:T(4,128)S(1)}, s32[128,4]{0,1:T(4,128)}, u32[]{:S(2)}) copy-start(s32[128,4]{0,1:T(4,128)} %param.10) | copy-start | bytes 6148
  0.7 19.1 %copy-start.4 = (f32[3,8,32,256]{3,2,1,0:T(8,128)S(1)}, f32[3,8,32,256]{3,2,1,0:T(8,128)}, u32[]{:S(2)}) copy-start(f32[3,8,32,256]{3,2,1,0:T(8,128)} %param.7) | copy-start | bytes 2359300
  0.7 121.7 %copy-start.11 = (f32[8,32,256]{2,1,0:T(8,128)S(1)}, f32[8,32,256]{2,1,0:T(8,128)}, u32[]{:S(2)}) copy-start(f32[8,32,256]{2,1,0:T(8,128)} %param.8) | copy-start | bytes 786436
  2.8 119.6 %collective-permute-start = (f32[4,3,32,256]{3,2,1,0:T(8,128)}, f32[4,3,32,256]{3,2,1,0:T(8,128)S(1)}, u32[]{:S(2)}, u32[]{:S(2)}) collective-permute-start(f32[4,3,32,256]{3,2,1,0:T(8,128)} %get-tuple-element.37), channel_id=1, source_target_pairs={{0,4},{4,8},{8,12},{12,16},{16,20},{20,24},{24,28},{28,32},{32,36}... | collective-permute-start | bytes 1179656 | tf_op jit(solution)/shard_map/ppermute | solution.py:22
  7.6 114.8 %collective-permute-start.1 = (f32[4,3,32,256]{3,2,1,0:T(8,128)S(1)}, f32[4,3,32,256]{3,2,1,0:T(8,128)S(1)}, u32[]{:S(2)}, u32[]{:S(2)}) collective-permute-start(f32[4,3,32,256]{3,2,1,0:T(8,128)S(1)} %get-tuple-element.38), channel_id=1, source_target_pairs={{4,0},{8,4},{12,8},{16,12},{20,16},{24,20},{28,24},{32,28},{36,32}... | collective-permute-start | bytes 1179656 | tf_op jit(solution)/shard_map/ppermute | solution.py:25
  122.5 9.4 %collective-permute-start.2 = (f32[4,14,3,256]{3,2,1,0:T(4,128)S(1)}, f32[4,14,3,256]{3,2,1,0:T(4,128)S(1)}, u32[]{:S(2)}, u32[]{:S(2)}) collective-permute-start(f32[4,14,3,256]{3,2,1,0:T(4,128)S(1)} %get-tuple-element.29), channel_id=1, source_target_pairs={{0,1},{1,2},{2,3},{4,5},{5,6},{6,7},{8,9},{9,10},{10,11},{12,13},{... | collective-permute-start | bytes 516104 | tf_op jit(solution)/shard_map/ppermute | solution.py:22
  129.0 11.9 %collective-permute-start.3 = (f32[4,14,3,256]{3,2,1,0:T(4,128)S(1)}, f32[4,14,3,256]{3,2,1,0:T(4,128)S(1)}, u32[]{:S(2)}, u32[]{:S(2)}) collective-permute-start(f32[4,14,3,256]{3,2,1,0:T(4,128)S(1)} %get-tuple-element.30), channel_id=1, source_target_pairs={{1,0},{2,1},{3,2},{5,4},{6,5},{7,6},{9,8},{10,9},{11,10},{13,12},{... | collective-permute-start | bytes 516104 | tf_op jit(solution)/shard_map/ppermute | solution.py:25
  140.9 4.1 %copy-start.6 = (f32[14,38,256]{2,1,0:T(8,128)}, f32[14,38,256]{2,1,0:T(8,128)S(1)}, u32[]{:S(2)}) copy-start(f32[14,38,256]{2,1,0:T(8,128)S(1)} %get-tuple-element.6) | copy-start | bytes 1634308
  143.8 1.3 copy-start.8
  143.8 1.3 copy-start.9
  144.7 0.8 copy-start.10
  145.1 3.0 copy-start.2
  148.0 21.4 %copy-start.1 = (f32[3,14,38,256]{3,2,1,0:T(8,128)}, f32[3,14,38,256]{3,2,1,0:T(8,128)S(1)}, u32[]{:S(2)}) copy-start(f32[3,14,38,256]{3,2,1,0:T(8,128)S(1)} %get-tuple-element.9) | copy-start | bytes 4902916
  173.7 4.2 %copy-start.7 = (f32[14,38,256]{2,1,0:T(8,128)S(1)}, f32[14,38,256]{2,1,0:T(8,128)}, u32[]{:S(2)}) copy-start(f32[14,38,256]{2,1,0:T(8,128)} %copy-done.6) | copy-start | bytes 1634308
  204.3 27.9 %copy-start.3 = (f32[3,14,38,256]{3,2,1,0:T(8,128)}, f32[3,14,38,256]{3,2,1,0:T(8,128)S(1)}, u32[]{:S(2)}) copy-start(f32[3,14,38,256]{3,2,1,0:T(8,128)S(1)} %get-tuple-element.39) | copy-start | bytes 4902916
  204.3 10.7 %collective-permute-start.4 = (f32[3,3,38,256]{3,2,1,0:T(8,128)S(1)}, f32[3,3,38,256]{3,2,1,0:T(8,128)S(1)}, u32[]{:S(2)}, u32[]{:S(2)}) collective-permute-start(f32[3,3,38,256]{3,2,1,0:T(8,128)S(1)} %slice.1414), channel_id=1, source_target_pairs={{4,0},{8,4},{12,8},{16,12},{20,16},{24,20},{28,24},{32,28},{36,32}... | collective-permute-start | bytes 1050632 | tf_op jit(solution)/shard_map/ppermute | solution.py:33
  215.1 15.0 %collective-permute-start.5 = (f32[3,3,38,256]{3,2,1,0:T(8,128)S(1)}, f32[3,3,38,256]{3,2,1,0:T(8,128)S(1)}, u32[]{:S(2)}, u32[]{:S(2)}) collective-permute-start(f32[3,3,38,256]{3,2,1,0:T(8,128)S(1)} %get-tuple-element.33), channel_id=1, source_target_pairs={{508,0},{0,4},{4,8},{8,12},{12,16},{16,20},{20,24},{24,28},{28,32}... | collective-permute-start | bytes 1050632 | tf_op jit(solution)/shard_map/ppermute | solution.py:33
  230.3 14.8 %collective-permute-start.6 = (f32[3,8,3,256]{3,2,1,0:T(4,128)S(1)}, f32[3,8,3,256]{3,2,1,0:T(4,128)S(1)}, u32[]{:S(2)}, u32[]{:S(2)}) collective-permute-start(f32[3,8,3,256]{3,2,1,0:T(4,128)S(1)} %get-tuple-element.32), channel_id=1, source_target_pairs={{1,0},{2,1},{3,2},{5,4},{6,5},{7,6},{9,8},{10,9},{11,10},{13,12},{... | collective-permute-start | bytes 221192 | tf_op jit(solution)/shard_map/ppermute | solution.py:39
  237.5 9.2 %collective-permute-start.7 = (f32[3,8,3,256]{3,2,1,0:T(4,128)S(1)}, f32[3,8,3,256]{3,2,1,0:T(4,128)S(1)}, u32[]{:S(2)}, u32[]{:S(2)}) collective-permute-start(f32[3,8,3,256]{3,2,1,0:T(4,128)S(1)} %get-tuple-element.31), channel_id=1, source_target_pairs={{0,1},{1,2},{2,3},{4,5},{5,6},{6,7},{8,9},{9,10},{10,11},{12,13},{... | collective-permute-start | bytes 221192 | tf_op jit(solution)/shard_map/ppermute | solution.py:39
where the time goes:
time: 347 us; the launch traced here: 346 us
  blocking collectives  195 us (56%)
  other arithmetic  76.1 us (22%)
  starting transfers between devices  41.6 us (12%)
  waiting for transfers between devices  26.5 us (8%)
    psum x1, blocking collectives, body(): lax.psum(block_means[:, None] * my_pick[None, :], ('wide', 'narrow'))  102 us
    pmax x1, blocking collectives, body(): largest = lax.pmax(jnp.max(jnp.abs(sens_raw)), ('wide', 'narrow'))  93.6 us
    sub x5, other arithmetic, apply_operator(): 6.0 * centre - beside + penalty_box * centre - GRAD_DIV_WEIGHT * grad_div  51.6 us
    ppermute x2, waiting for transfers between devices, passed_along(): return lax.ppermute(block, axis, route)  15.3 us
    ppermute x2, starting transfers between devices, extended_2(): lax.ppermute(lax.slice_in_dim(block, 0, width, axis=dim), axis, backward)  12.6 us
    ppermute x2, starting transfers between devices, extended_2(): lax.ppermute(lax.slice_in_dim(block, block.shape[dim] - width, None, axis...  11.2 us
    mul x3, other arithmetic, local_solve(): inside * (iterate + DAMPING * (source - apply_operator(iterate, penalty_b...  9.73 us
    ppermute x2, starting transfers between devices, passed_along_2(): lax.ppermute(value, axis, [(source, source + steps) for source in range(i...  9.47 us
  transfers between devices with their start and end apart: 8, of which 5 were waited for; matrix products, arithmetic and copies ran while one was open for 3% of the time, Pallas kernels for 0%

commit v1 on v0

v1 whole, which is shorter than its diff:
```python
import functools

import jax
import jax.numpy as jnp
from jax import lax
from jax.experimental import pallas as pl
from jax.experimental.pallas import tpu as pltpu
from jax.sharding import PartitionSpec as P

MESH = pl.DeviceIdType.MESH
F32 = jnp.float32

OV = 3
CX = 8
CY = 32
LANES = 128
GROUPS = 64
W = 128
N = 4
DAMPING = 0.7
PEAK_EPS = 1e-06

XR = 16
YR = 48
X0 = 4
Y0 = 8
BOX_Y = 5
BOX_NY = 40
PEN, STATE = 0, 1


def zshift(v0, v1, lane):
    a0, a1 = pltpu.roll(v0, LANES - 1, 1), pltpu.roll(v1, LANES - 1, 1)
    b0, b1 = pltpu.roll(v0, 1, 1), pltpu.roll(v1, 1, 1)
    last, first = lane == LANES - 1, lane == 0
    return (
        (jnp.where(last, a1, a0), jnp.where(first, 0.0, b0)),
        (jnp.where(last, 0.0, a1), jnp.where(first, b0, b1)),
    )


def sweep(src, dst, source, gain, tx, ty, lo, hi):
    y0, ny = BOX_Y, BOX_NY
    lane = lax.broadcasted_iota(jnp.int32, (ny, LANES), 1)

    def at(ref, h, c, i, d=0):
        return ref[h, c, i, pl.ds(y0 + d, ny), :]

    def flat(ref, h, i, d=0):
        return ref[h, i, pl.ds(y0 + d, ny), :]

    def edge(i):
        for h, (plus, minus) in enumerate(zshift(at(src, 0, 2, i), at(src, 1, 2, i), lane)):
            q = at(src, h, 1, i, 1) - at(src, h, 1, i, -1)
            tx[h, i, pl.ds(y0, ny), :] = 0.25 * (q + (plus - minus))

    def first(i, carry):
        vz = [at(src, h, 2, i) for h in (0, 1)]
        mixed, sums = [], []
        for h, (plus, minus) in enumerate(zshift(vz[0], vz[1], lane)):
            p = at(src, h, 0, i + 1) - at(src, h, 0, i - 1)
            q = at(src, h, 1, i, 1) - at(src, h, 1, i, -1)
            r = plus - minus
            tx[h, i, pl.ds(y0, ny), :] = 0.25 * (q + r)
            ty[h, i, pl.ds(y0, ny), :] = 0.25 * (p + r)
            mixed.append(0.25 * (p + q))
            own = plus + minus
            sums.append(
                (own + own)
                + (at(src, h, 2, i + 1) + at(src, h, 2, i - 1))
                + (at(src, h, 2, i, 1) + at(src, h, 2, i, -1))
            )
        for h, (plus, minus) in enumerate(zshift(mixed[0], mixed[1], lane)):
            total = at(source, h, 2, i) + (sums[h] + (plus - minus))
            dst[h, 2, i, pl.ds(y0, ny), :] = 0.3 * vz[h] + flat(gain, h, i) * total
        return carry

    def second(i, carry):
        vx = [at(src, h, 0, i) for h in (0, 1)]
        vy = [at(src, h, 1, i) for h in (0, 1)]
        zx = zshift(vx[0], vx[1], lane)
        zy = zshift(vy[0], vy[1], lane)
        for h in (0, 1):
            g = flat(gain, h, i)
            own = at(src, h, 0, i + 1) + at(src, h, 0, i - 1)
            total = (
                (own + own)
                + (at(src, h, 0, i, 1) + at(src, h, 0, i, -1))
                + (zx[h][0] + zx[h][1])
                + (flat(tx, h, i + 1) - flat(tx, h, i - 1))
            )
            dst[h, 0, i, pl.ds(y0, ny), :] = 0.3 * vx[h] + g * (at(source, h, 0, i) + total)
            own = at(src, h, 1, i, 1) + at(src, h, 1, i, -1)
            total = (
                (own + own)
                + (at(src, h, 1, i + 1) + at(src, h, 1, i - 1))
                + (zy[h][0] + zy[h][1])
                + (flat(ty, h, i, 1) - flat(ty, h, i, -1))
            )
            dst[h, 1, i, pl.ds(y0, ny), :] = 0.3 * vy[h] + g * (at(source, h, 1, i) + total)
        return carry

    edge(lo - 1)
    edge(hi + 1)
    lax.fori_loop(lo, hi + 1, first, 0)
    lax.fori_loop(lo, hi + 1, second, 0)


def zero(ref):
    lead = ref.shape[:-3]
    rows = ref.shape[-2:]

    def one(i, carry):
        for h in range(lead[0]):
            if len(lead) == 1:
                ref[h, i] = jnp.zeros(rows, F32)
            else:
                for c in range(lead[1]):
                    ref[h, c, i] = jnp.zeros(rows, F32)
        return carry

    lax.fori_loop(0, ref.shape[-3], one, 0)


def zero_margins(ref):
    def one(i, carry):
        for h in (0, 1):
            for y in (0, Y0 + CY):
                if len(ref.shape) == 4:
                    ref[h, i, pl.ds(y, 8), :] = jnp.zeros((8, LANES), F32)
                else:
                    for c in range(3):
                        ref[h, c, i, pl.ds(y, 8), :] = jnp.zeros((8, LANES), F32)
        return carry

    lax.fori_loop(0, XR, one, 0)


def kernel(
    state,
    adjoint,
    penalty,
    margin,
    owner,
    inverse,
    state_out,
    adjoint_out,
    sens_out,
    s_src,
    a_src,
    s_a,
    s_b,
    a_a,
    a_b,
    pen,
    gain,
    tx,
    ty,
    py_out,
    py_in,
    pc_out,
    pc_in,
    sy_out,
    sy_in,
    sc_out,
    sc_in,
    ay_out,
    ay_in,
    ax_in,
    red,
    corr,
    load_sem,
    x_send,
    x_recv,
    y_send,
    y_recv,
    r_send,
    r_recv,
):
    w, n = lax.axis_index("wide"), lax.axis_index("narrow")
    py, px, pz = w // 16, lax.rem(w // 4, 4), lax.rem(w, 4)
    ph, pc = n // 2, lax.rem(n, 2)
    left, right = lax.rem(w + W - 1, W), lax.rem(w + 1, W)
    down, up = lax.rem(n + N - 1, N), lax.rem(n + 1, N)
    stages = (
        [(lax.rem(py + k, 8) * 16 + px * 4 + pz, n) for k in range(1, 8)],
        [
            (py * 16 + lax.rem(px + k // 2, 4) * 4 + pz, ph * 2 + lax.rem(pc + k % 2, 2))
            for k in range(1, 8)
        ],
        [
            (py * 16 + px * 4 + lax.rem(pz + k // 2, 4), lax.rem(ph + k % 2, 2) * 2 + pc)
            for k in range(1, 8)
        ],
    )
    has_down, has_up = n > 0, n < N - 1

    barrier = pltpu.get_barrier_semaphore()
    for device in [(left, n), (right, n)] + stages[0] + stages[1] + stages[2]:
        pl.semaphore_signal(barrier, inc=1, device_id=device, device_id_type=MESH)

    @pl.when(has_down)
    def _():
        pl.semaphore_signal(barrier, inc=1, device_id=(w, down), device_id_type=MESH)

    @pl.when(has_up)
    def _():
        pl.semaphore_signal(barrier, inc=1, device_id=(w, up), device_id_type=MESH)

    loads = []
    for h in (0, 1):
        z = pl.ds(h * LANES, LANES)
        own_x, own_y = pl.ds(X0, CX), pl.ds(Y0, CY)
        for k, (ref, target) in enumerate(
            (
                (penalty.at[:, :, z], pen.at[h, own_x, own_y, :]),
                (adjoint.at[:, :, :, z], a_src.at[h, :, own_x, own_y, :]),
                (state.at[:, :, :, z], s_src.at[h, :, own_x, own_y, :]),
            )
        ):
            copy = pltpu.make_async_copy(ref, target, load_sem.at[2 * k + h])
            copy.start()
            loads.append(copy)

    zero_margins(pen)
    zero_margins(s_src)
    zero_margins(a_src)
    for ref in (s_a, s_b, a_a, a_b, tx, ty):
        zero(ref)
    for h in (0, 1):
        for c in range(3):
            for x in (0, 1, 2, 3, 12, 13, 14, 15):
                a_src[h, c, x, pl.ds(Y0, CY), :] = jnp.zeros((CY, LANES), F32)

    peers = 23 + has_down.astype(jnp.int32) + has_up.astype(jnp.int32)
    pl.semaphore_wait(barrier, peers)

    def x_copy(which, d, h):
        rows, target = (pl.ds(0, OV), pl.ds(12, OV)) if d == 0 else (pl.ds(CX - OV, OV), pl.ds(1, OV))
        z, own_y = pl.ds(h * LANES, LANES), pl.ds(Y0, CY)
        if which == PEN:
            ref, to = penalty.at[rows, :, z], pen.at[h, target, own_y, :]
        else:
            ref, to = state.at[:, rows, :, z], s_src.at[h, :, target, own_y, :]
        return pltpu.make_async_remote_copy(
            src_ref=ref,
            dst_ref=to,
            send_sem=x_send.at[4 * which + 2 * d + h],
            recv_sem=x_recv.at[4 * which + 2 * (1 - d) + h],
            device_id=(left if d == 0 else right, n),
            device_id_type=MESH,
        )

    def adjoint_copy(d, h):
        rows = pl.ds(1, OV) if d == 0 else pl.ds(12, OV)
        return pltpu.make_async_remote_copy(
            src_ref=a_b.at[h, :, rows, pl.ds(Y0, CY), :],
            dst_ref=ax_in.at[1 - d, h],
            send_sem=x_send.at[8 + 2 * d + h],
            recv_sem=x_recv.at[8 + 2 * (1 - d) + h],
            device_id=(left if d == 0 else right, n),
            device_id_type=MESH,
        )

    both = [(d, h) for d in (0, 1) for h in (0, 1)]
    for which in (PEN, STATE):
        for d, h in both:
            x_copy(which, d, h).start()

    def y_copy(message, d):
        out, land = ((py_out, py_in), (pc_out, pc_in), (sy_out, sy_in), (sc_out, sc_in), (ay_out, ay_in))[
            message
        ]
        return pltpu.make_async_remote_copy(
            src_ref=out.at[d],
            dst_ref=land.at[1 - d],
            send_sem=y_send.at[2 * message + d],
            recv_sem=y_recv.at[2 * message + 1 - d],
            device_id=(w, down if d == 0 else up),
            device_id_type=MESH,
        )

    def each_side(action):
        @pl.when(has_down)
        def _():
            action(0)

        @pl.when(has_up)
        def _():
            action(1)

    def y_send_now(message):
        each_side(lambda d: y_copy(message, d).start())

    inner = (Y0, Y0 + CY - OV)
    outer = (Y0 - OV, Y0 + CY)

    def rows_of(ref, h, c, i, y):
        return ref.at[h, i, pl.ds(y, OV), :] if c is None else ref.at[h, c, i, pl.ds(y, OV), :]

    def moves(blocks, comps, step):
        width = sum(count for _, count in blocks)
        base = 0
        for start, count in blocks:

            def one(k, carry, start=start, base=base):
                for h in (0, 1):
                    for j, c in enumerate(comps):
                        step(h, c, start + k, pl.ds((j * width + base + k) * OV, OV))
                return carry

            lax.fori_loop(0, count, one, 0)
            base += count

    def pack(ref, out, blocks, comps, d, ys):
        def step(h, c, i, slot):
            out[d, h, slot, :] = rows_of(ref, h, c, i, ys[d])[...]

        moves(blocks, comps, step)

    def unpack(ref, land, blocks, comps, d, ys, add=False):
        def step(h, c, i, slot):
            cell = rows_of(ref, h, c, i, ys[d])
            cell[...] = cell[...] + land[d, h, slot, :] if add else land[d, h, slot, :]

        moves(blocks, comps, step)

    own_rows = ((X0, CX),)
    rim_rows = ((1, OV), (12, OV))
    box_rows = ((1, CX + 2 * OV),)
    pen_comps, all_comps = (None,), (0, 1, 2)

    def reduce_copy(use, s, k):
        slot = (use * 3 + s) * 8
        return pltpu.make_async_remote_copy(
            src_ref=red.at[slot],
            dst_ref=red.at[slot + k],
            send_sem=r_send.at[slot + k],
            recv_sem=r_recv.at[slot + k],
            device_id=stages[s][k - 1],
            device_id_type=MESH,
        )

    def reduce_start(use, s, value):
        red[(use * 3 + s) * 8] = value
        for k in range(1, 8):
            reduce_copy(use, s, k).start()

    def reduce_finish(use, s, combine):
        for k in range(1, 8):
            reduce_copy(use, s, k).wait_recv()
        slot = (use * 3 + s) * 8
        value = [red[slot + k] for k in range(8)]
        while len(value) > 1:
            value = [combine(value[2 * k], value[2 * k + 1]) for k in range(len(value) // 2)]
        return value[0]

    for copy in loads:
        copy.wait()

    each_side(lambda d: pack(pen, py_out, own_rows, pen_comps, d, inner))
    y_send_now(0)
    each_side(lambda d: pack(s_src, sy_out, own_rows, all_comps, d, inner))
    y_send_now(2)

    spot = (lax.broadcasted_iota(jnp.int32, (N, W), 0) == n) & (
        lax.broadcasted_iota(jnp.int32, (N, W), 1) == w
    )
    own_group = jnp.sum(jnp.where(spot, owner[...].astype(F32), 0.0), axis=(0, 1), keepdims=True)
    pick = (lax.broadcasted_iota(jnp.int32, (1, LANES), 1).astype(F32) == own_group).astype(F32)
    row = lax.broadcasted_iota(jnp.int32, (8, LANES), 0)
    sums = jnp.zeros((8, LANES), F32)
    for k, ref in enumerate((s_src, a_src)):
        for c in range(3):

            def add(i, total, ref=ref, c=c):
                cells = ref[0, c, i, pl.ds(Y0, CY), :] + ref[1, c, i, pl.ds(Y0, CY), :]
                return total + ((cells[0:8] + cells[8:16]) + (cells[16:24] + cells[24:32]))

            total = lax.fori_loop(X0, X0 + CX, add, jnp.zeros((8, LANES), F32))
            mean = jnp.sum(total, axis=(0, 1), keepdims=True) * (1.0 / (CX * CY * 2 * LANES))
            sums = sums + jnp.where(row == 3 * k + c, mean * pick, 0.0)
    reduce_start(0, 0, sums)

    for d, h in both:
        x_copy(PEN, d, h).wait_recv()
    each_side(lambda d: pack(pen, pc_out, rim_rows, pen_comps, d, inner))
    y_send_now(1)

    width = margin[0, 0]
    column = lax.broadcasted_iota(jnp.int32, (BOX_NY, LANES), 0) + (BOX_Y - Y0)
    place = column + n * CY
    in_y = (column >= -width) & (column < CY + width) & (place >= 0) & (place < N * CY)

    def y_arrived(message, d):
        y_copy(message, 1 - d).wait_recv()

    each_side(lambda d: y_arrived(0, d))
    each_side(lambda d: unpack(pen, py_in, own_rows, pen_comps, d, outer))
    each_side(lambda d: y_arrived(1, d))
    each_side(lambda d: unpack(pen, pc_in, rim_rows, pen_comps, d, outer))

    def set_gain(i, carry):
        line = jnp.zeros((BOX_NY, LANES), jnp.int32) + (i - X0)
        inside = in_y & (line >= -width) & (line < CX + width)
        for h in (0, 1):
            value = DAMPING / (8.0 + pen[h, i, pl.ds(BOX_Y, BOX_NY), :])
            gain[h, i, pl.ds(BOX_Y, BOX_NY), :] = jnp.where(inside, value, 0.0)
        return carry

    lax.fori_loop(1, XR - 1, set_gain, 0)

    def adjoint_first(i, carry):
        for h in (0, 1):
            g = gain[h, i, pl.ds(Y0, CY), :]
            for c in range(3):
                a_a[h, c, i, pl.ds(Y0, CY), :] = g * a_src[h, c, i, pl.ds(Y0, CY), :]
        return carry

    lax.fori_loop(X0, X0 + CX, adjoint_first, 0)
    sweep(a_a, a_b, a_src, gain, tx, ty, 3, 12)
    total = reduce_finish(0, 0, jnp.add)
    reduce_start(0, 1, total)
    sweep(a_b, a_a, a_src, gain, tx, ty, 2, 13)
    total = reduce_finish(0, 1, jnp.add)
    reduce_start(0, 2, total)
    sweep(a_a, a_b, a_src, gain, tx, ty, 1, 14)

    each_side(lambda d: pack(a_b, ay_out, box_rows, all_comps, d, outer))
    y_send_now(4)

    for d, h in both:
        x_copy(STATE, d, h).wait_recv()
    each_side(lambda d: pack(s_src, sc_out, rim_rows, all_comps, d, inner))
    y_send_now(3)

    each_side(lambda d: y_arrived(4, d))
    each_side(lambda d: unpack(a_b, ay_in, box_rows, all_comps, d, inner, add=True))
    for d, h in both:
        adjoint_copy(d, h).start()

    coarse = reduce_finish(0, 2, jnp.add)
    inv = inverse[...]
    across = lax.broadcasted_iota(jnp.int32, (GROUPS, GROUPS), 1)
    along = lax.broadcasted_iota(jnp.int32, (GROUPS, GROUPS), 0)
    rhs = coarse[:, :GROUPS]
    state_row = jnp.sum(
        ((along.astype(F32) == own_group).astype(F32) - 1.0 / GROUPS) * inv, axis=0, keepdims=True
    )
    adjoint_column = jnp.sum(
        (across.astype(F32) == own_group).astype(F32) * inv, axis=1, keepdims=True
    )
    adjoint_row = jnp.sum(jnp.where(along == across, adjoint_column, 0.0), axis=0, keepdims=True)
    centred = rhs - jnp.sum(rhs, axis=1, keepdims=True) * (1.0 / GROUPS)
    by_state = jnp.sum(rhs * state_row, axis=1, keepdims=True)
    by_adjoint = jnp.sum(centred * adjoint_row, axis=1, keepdims=True)
    corr[...] = jnp.where(row < 3, by_state, by_adjoint)

    for message in (2, 3):
        blocks = own_rows if message == 2 else rim_rows
        land = sy_in if message == 2 else sc_in
        each_side(lambda d, message=message: y_arrived(message, d))
        each_side(lambda d, blocks=blocks, land=land: unpack(s_src, land, blocks, all_comps, d, outer))

    def state_first(i, carry):
        for h in (0, 1):
            g = gain[h, i, pl.ds(BOX_Y, BOX_NY), :]
            for c in range(3):
                s_a[h, c, i, pl.ds(BOX_Y, BOX_NY), :] = g * s_src[h, c, i, pl.ds(BOX_Y, BOX_NY), :]
        return carry

    lax.fori_loop(1, XR - 1, state_first, 0)
    sweep(s_a, s_b, s_src, gain, tx, ty, 2, 13)
    sweep(s_b, s_a, s_src, gain, tx, ty, 3, 12)
    sweep(s_a, s_b, s_src, gain, tx, ty, 4, 11)

    for d, h in both:
        adjoint_copy(d, h).wait_recv()

    def add_shares(k, carry):
        for h in (0, 1):
            for c in range(3):
                for d, x in ((0, X0), (1, X0 + CX - OV)):
                    a_b[h, c, x + k, pl.ds(Y0, CY), :] = (
                        a_b[h, c, x + k, pl.ds(Y0, CY), :] + ax_in[d, h, c, k]
                    )
        return carry

    for d, h in both:
        adjoint_copy(d, h).wait_send()
    lax.fori_loop(0, OV, add_shares, 0)

    def finish(i, peak):
        for h in (0, 1):
            z = slice(h * LANES, (h + 1) * LANES)
            raw = None
            for c in range(3):
                s = s_b[h, c, X0 + i, pl.ds(Y0, CY), :] + corr[pl.ds(c, 1), :]
                a = a_b[h, c, X0 + i, pl.ds(Y0, CY), :] + corr[pl.ds(c + 3, 1), :]
                state_out[c, i, :, z] = s
                adjoint_out[c, i, :, z] = a
                raw = s * a if raw is None else raw + s * a
            sens_out[i, :, z] = -raw
            size = jnp.abs(raw)
            peak = jnp.maximum(
                peak,
                jnp.maximum(jnp.maximum(size[0:8], size[8:16]), jnp.maximum(size[16:24], size[24:32])),
            )
        return peak

    peak = lax.fori_loop(0, CX, finish, jnp.zeros((8, LANES), F32))
    for s in range(3):
        reduce_start(1, s, peak)
        peak = reduce_finish(1, s, jnp.maximum)
    scale = 1.0 / (jnp.max(peak, axis=(0, 1), keepdims=True) + PEAK_EPS)

    def normalise(i, carry):
        sens_out[i] = sens_out[i] * scale
        return carry

    lax.fori_loop(0, CX, normalise, 0)

    for which in (PEN, STATE):
        for d, h in both:
            x_copy(which, d, h).wait_send()
    for message in range(5):
        each_side(lambda d, message=message: y_copy(message, d).wait_send())
    for use in (0, 1):
        for s in range(3):
            for k in range(1, 8):
                reduce_copy(use, s, k).wait_send()


def body(state_rhs, adjoint_rhs, penalty, margin_width, owner_map, coarse_inv):
    vmem = pltpu.VMEM
    field = vmem((2, 3, XR, YR, LANES), F32)
    flat = vmem((2, XR, YR, LANES), F32)

    def message(rows):
        return [vmem((2, 2, rows, LANES), F32)] * 2

    dma = pltpu.SemaphoreType.DMA
    return pl.pallas_call(
        kernel,
        out_shape=(
            jax.ShapeDtypeStruct(state_rhs.shape, F32),
            jax.ShapeDtypeStruct(adjoint_rhs.shape, F32),
            jax.ShapeDtypeStruct(penalty.shape, F32),
        ),
        in_specs=[pl.BlockSpec(memory_space=pl.ANY)] * 3
        + [pl.BlockSpec(memory_space=pltpu.SMEM)]
        + [pl.BlockSpec(memory_space=vmem)] * 2,
        out_specs=(pl.BlockSpec(memory_space=vmem),) * 3,
        scratch_shapes=[field] * 6
        + [flat] * 4
        + message(24)
        + message(24)
        + message(72)
        + message(56)
        + message(128)
        + [
            vmem((2, 2, 3, OV, CY, LANES), F32),
            vmem((48, 8, LANES), F32),
            vmem((8, LANES), F32),
            dma((6,)),
            dma((12,)),
            dma((12,)),
            dma((10,)),
            dma((10,)),
            dma((48,)),
            dma((48,)),
        ],
        compiler_params=pltpu.CompilerParams(
            collective_id=0, has_side_effects=True, vmem_limit_bytes=60 * 1024 * 1024
        ),
        name="schwarz",
    )(state_rhs, adjoint_rhs, penalty, margin_width, owner_map.T, coarse_inv)


def solution(mesh):
    placed = (
        P(None, "wide", "narrow", None),
        P(None, "wide", "narrow", None),
        P("wide", "narrow", None),
        P("wide", "narrow"),
        P(),
        P(),
    )
    return jax.shard_map(
        body,
        mesh=mesh,
        in_specs=placed,
        out_specs=(
            P(None, "wide", "narrow", None),
            P(None, "wide", "narrow", None),
            P("wide", "narrow", None),
        ),
        check_vma=False,
    )
```

time: 347 us -> 91.6 us (0.26)
  blocking collectives: 195 us -> 0 us
  Pallas kernels: 0 us -> 86.1 us
  other arithmetic: 76.1 us -> 0 us
  starting transfers between devices: 41.6 us -> 0 us
  waiting for transfers between devices: 26.5 us -> 0 us
    psum x1 -> x0, blocking collectives: 102 us -> none  [body(): lax.psum(block_means[:, None] * my_pick[None, :], ('wide', 'narrow'))]
    pmax x1 -> x0, blocking collectives: 93.6 us -> none  [body(): largest = lax.pmax(jnp.max(jnp.abs(sens_raw)), ('wide', 'narrow'))]
    pallas_call x0 -> x1, Pallas kernels: none -> 86.1 us  [body(): pl.pallas_call(kernel, out_shape=(jax.ShapeDtypeStruct(state_rhs.shape, F...]
    sub x5 -> x0, other arithmetic: 51.6 us -> none  [apply_operator(): 6.0 * centre - beside + penalty_box * centre - GRAD_DIV_WEIGHT * grad_div]
    ppermute x8 -> x0, starting transfers between devices: 41.6 us -> none  [the longest x2 12.6 us: extended_2(): lax.ppermute(lax.slice_in_dim(block, 0, width, axis=dim), axis, backward)]
    ppermute x8 -> x0, waiting for transfers between devices: 26.5 us -> none  [the longest x2 15.3 us: passed_along(): return lax.ppermute(block, axis, route)]
    mul x5 -> x0, other arithmetic: 12.3 us -> none  [the longest x3 9.73 us: local_solve(): inside * (iterate + DAMPING * (source - apply_operator(iterate, penalty_b...]
    reduce_sum x5 -> x0, other arithmetic: 4.41 us -> none  [the longest x1 3.31 us: body(): sens_raw = -jnp.sum(state_update * adjoint_update, axis=0)]
  transfers between devices with their start and end apart: 8 -> 0, of which waited for: 5 -> 0; matrix products, arithmetic and copies ran while one was open for 3% -> 0% of each run, Pallas kernels for 0% -> 0%
where the time goes in v1:
time: 91.6 us; the launch traced here: 91.3 us
  Pallas kernels  86.1 us (94%)
  local copies, waits for them, and re-layouts  3.96 us (4%)
  between operations  1.3 us (1%)
    pallas_call x1, Pallas kernels, body(): pl.pallas_call(kernel, out_shape=(jax.ShapeDtypeStruct(state_rhs.shape, F...  86.1 us
    unnamed x7, local copies, waits for them, and re-layouts  3.96 us

profile of v1, /device:TPU:1, one launch (start us, length us, event | category | flops | bytes accessed | tf_op | source)
XLA Modules:
  0.0 91.3 jit_solution(253781953218599820)
XLA Ops:
  1.3 86.1 %schwarz.1 = (f32[3,8,32,256]{3,2,1,0:T(8,128)}, f32[3,8,32,256]{3,2,1,0:T(8,128)}, f32[8,32,256]{2,1,0:T(8,128)}) custom-call(f32[3,8,32,256]{3,2,1,0:T(8,128)} %state.1, f32[3,8,32,256]{3,2,1,0:T(8,128)} %adjoint.1, f32[8,32,256]{2,1,0:T(8,128)} %penalty.1, s32[1,1]{1,0:T(1,128)S(6)} %copy.12.margin, s32[4,128]{1,0:T(4,128)} %bitcast.1, f32[64,64]{1,0:T(8,128)} %inverse.1), custom_call_target="tpu_custom_call" | custom-call | tf_op jit(solution)/shard_map/schwarz/pallas_call | solution.py:543
  87.4 0.0 copy-start
  87.4 2.2 %copy.13 = f32[3,8,32,256]{3,2,1,0:T(8,128)} copy(f32[3,8,32,256]{3,2,1,0:T(8,128)} %get-tuple-element.6) | data formatting | bytes 1572864
  89.5 0.0 copy-done
  89.5 0.0 copy-start.1
  89.5 0.9 copy.14
  90.4 0.2 copy-done.1
  90.6 0.7 copy.15
Async XLA Ops:
  87.4 2.2 %copy-start = (f32[3,8,32,256]{3,2,1,0:T(8,128)S(1)}, f32[3,8,32,256]{3,2,1,0:T(8,128)}, u32[]{:S(2)}) copy-start(f32[3,8,32,256]{3,2,1,0:T(8,128)} %get-tuple-element.7) | copy-start | bytes 2359300
  89.5 1.1 %copy-start.1 = (f32[8,32,256]{2,1,0:T(8,128)S(1)}, f32[8,32,256]{2,1,0:T(8,128)}, u32[]{:S(2)}) copy-start(f32[8,32,256]{2,1,0:T(8,128)} %get-tuple-element.8) | copy-start | bytes 786436

commit v2 on v1

v2 whole, which is shorter than its diff:
```python
import functools

import jax
import jax.numpy as jnp
from jax import lax
from jax.experimental import pallas as pl
from jax.experimental.pallas import tpu as pltpu
from jax.sharding import PartitionSpec as P

MESH = pl.DeviceIdType.MESH
F32 = jnp.float32

OV = 3
CX = 8
CY = 32
LANES = 128
GROUPS = 64
W = 128
N = 4
DAMPING = 0.7
PEAK_EPS = 1e-06

XR = 16
YR = 48
X0 = 4
Y0 = 8
BOX_Y = 5
BOX_NY = 40
PEN, STATE = 0, 1


def next_and_previous(plus, minus, lane):
    a0, a1 = pltpu.roll(plus[0], LANES - 1, 1), pltpu.roll(plus[1], LANES - 1, 1)
    b0, b1 = pltpu.roll(minus[0], 1, 1), pltpu.roll(minus[1], 1, 1)
    last, first = lane == LANES - 1, lane == 0
    return (
        jnp.where(last, a1, a0) + jnp.where(first, 0.0, b0),
        jnp.where(last, 0.0, a1) + jnp.where(first, b0, b1),
    )


def sweep(src, dst, source, gain, lo, hi, y0=BOX_Y, ny=BOX_NY):
    lane = lax.broadcasted_iota(jnp.int32, (ny, LANES), 1)

    def line(i, carry):
        centre, plus, minus, rest = [], [], [], []
        for h in (0, 1):

            def at(c, di=0, dy=0, h=h):
                return src[h, c, i + di, pl.ds(y0 + dy, ny), :]

            x0, x1, x2 = at(0), at(0, 1), at(0, -1)
            y_0, y1, y2 = at(1), at(1, 0, 1), at(1, 0, -1)
            z0 = at(2)
            xz = 0.25 * (at(2, 1) - at(2, -1))
            yz = 0.25 * (at(2, 0, 1) - at(2, 0, -1))
            zz = 0.25 * ((x1 - x2) + (y1 - y2))
            twice = z0 + z0
            centre.append((x0, y_0, z0))
            plus.append((x0 + xz, y_0 + yz, twice + zz))
            minus.append((x0 - xz, y_0 - yz, twice - zz))
            own_x, own_y = x1 + x2, y1 + y2
            rest.append(
                (
                    (own_x + own_x)
                    + (at(0, 0, 1) + at(0, 0, -1))
                    + 0.25 * ((at(1, 1, 1) - at(1, 1, -1)) - (at(1, -1, 1) - at(1, -1, -1))),
                    (own_y + own_y)
                    + (at(1, 1) + at(1, -1))
                    + 0.25 * ((at(0, 1, 1) - at(0, 1, -1)) - (at(0, -1, 1) - at(0, -1, -1))),
                    (at(2, 1) + at(2, -1)) + (at(2, 0, 1) + at(2, 0, -1)),
                )
            )
        for c in range(3):
            along = next_and_previous((plus[0][c], plus[1][c]), (minus[0][c], minus[1][c]), lane)
            for h in (0, 1):
                total = source[h, c, i, pl.ds(y0, ny), :] + (rest[h][c] + along[h])
                g = gain[h, i, pl.ds(y0, ny), :]
                dst[h, c, i, pl.ds(y0, ny), :] = 0.3 * centre[h][c] + g * total
        return carry

    lax.fori_loop(lo, hi + 1, line, 0)


def zero_rows(ref, rows):
    for i in rows:
        for h in (0, 1):
            for c in range(3):
                ref[h, c, i] = jnp.zeros((YR, LANES), F32)


def zero_margins(ref):
    def one(i, carry):
        for h in (0, 1):
            for y in (0, Y0 + CY):
                if len(ref.shape) == 4:
                    ref[h, i, pl.ds(y, 8), :] = jnp.zeros((8, LANES), F32)
                else:
                    for c in range(3):
                        ref[h, c, i, pl.ds(y, 8), :] = jnp.zeros((8, LANES), F32)
        return carry

    lax.fori_loop(0, XR, one, 0)


def kernel(
    state,
    adjoint,
    penalty,
    margin,
    owner,
    inverse,
    state_out,
    adjoint_out,
    sens_out,
    s_src,
    a_src,
    s_a,
    s_b,
    a_a,
    a_b,
    pen,
    gain,
    py_out,
    py_in,
    pc_in,
    sy_out,
    sy_in,
    sc_out,
    sc_in,
    ay_out,
    ay_in,
    ac_out,
    ac_in,
    ax_in,
    total_red,
    peak_red,
    corr,
    load_sem,
    x_send,
    x_recv,
    y_send,
    y_recv,
    r_send,
    r_recv,
):
    w, n = lax.axis_index("wide"), lax.axis_index("narrow")
    py, px, pz = w // 16, lax.rem(w // 4, 4), lax.rem(w, 4)
    ph, pc = n // 2, lax.rem(n, 2)
    left, right = lax.rem(w + W - 1, W), lax.rem(w + 1, W)
    down, up = lax.rem(n + N - 1, N), lax.rem(n + 1, N)
    stages = (
        [
            (py * 16 + px * 4 + lax.rem(pz + k // 4, 4), lax.rem(ph + k // 2 % 2, 2) * 2 + lax.rem(pc + k % 2, 2))
            for k in range(1, 16)
        ],
        [(lax.rem(py + k // 4, 8) * 16 + lax.rem(px + k % 4, 4) * 4 + pz, n) for k in range(1, 32)],
    )
    has_down, has_up = n > 0, n < N - 1

    barrier = pltpu.get_barrier_semaphore()
    for device in [(left, n), (right, n)] + stages[0] + stages[1]:
        pl.semaphore_signal(barrier, inc=1, device_id=device, device_id_type=MESH)

    @pl.when(has_down)
    def _():
        for at in (left, w, right):
            pl.semaphore_signal(barrier, inc=1, device_id=(at, down), device_id_type=MESH)

    @pl.when(has_up)
    def _():
        for at in (left, w, right):
            pl.semaphore_signal(barrier, inc=1, device_id=(at, up), device_id_type=MESH)

    loads = []
    own_x, own_y = pl.ds(X0, CX), pl.ds(Y0, CY)
    for k in range(3):
        for h in (0, 1):
            z = pl.ds(h * LANES, LANES)
            ref, target = (
                (penalty.at[:, :, z], pen.at[h, own_x, own_y, :]),
                (adjoint.at[:, :, :, z], a_src.at[h, :, own_x, own_y, :]),
                (state.at[:, :, :, z], s_src.at[h, :, own_x, own_y, :]),
            )[k]
            copy = pltpu.make_async_copy(ref, target, load_sem.at[2 * k + h])
            copy.start()
            loads.append(copy)

    zero_margins(s_src)
    peers = 48 + 3 * (has_down.astype(jnp.int32) + has_up.astype(jnp.int32))
    pl.semaphore_wait(barrier, peers)

    def x_copy(which, d, h):
        rows, target = (pl.ds(0, OV), pl.ds(12, OV)) if d == 0 else (pl.ds(CX - OV, OV), pl.ds(1, OV))
        z, own_y = pl.ds(h * LANES, LANES), pl.ds(Y0, CY)
        if which == PEN:
            ref, to = penalty.at[rows, :, z], pen.at[h, target, own_y, :]
        else:
            ref, to = state.at[:, rows, :, z], s_src.at[h, :, target, own_y, :]
        return pltpu.make_async_remote_copy(
            src_ref=ref,
            dst_ref=to,
            send_sem=x_send.at[4 * which + 2 * d + h],
            recv_sem=x_recv.at[4 * which + 2 * (1 - d) + h],
            device_id=(left if d == 0 else right, n),
            device_id_type=MESH,
        )

    def adjoint_copy(d, h):
        rows = pl.ds(1, OV) if d == 0 else pl.ds(12, OV)
        return pltpu.make_async_remote_copy(
            src_ref=a_b.at[h, :, rows, pl.ds(Y0, CY), :],
            dst_ref=ax_in.at[1 - d, h],
            send_sem=x_send.at[8 + 2 * d + h],
            recv_sem=x_recv.at[8 + 2 * (1 - d) + h],
            device_id=(left if d == 0 else right, n),
            device_id_type=MESH,
        )

    both = [(d, h) for d in (0, 1) for h in (0, 1)]
    for d, h in both:
        x_copy(PEN, d, h).start()

    def y_copy(message, d):
        out, land, rows, side = messages[message]
        return pltpu.make_async_remote_copy(
            src_ref=out.at[d, :, rows, :],
            dst_ref=land.at[1 - d, :, rows, :] if side == 0 else land.at[1 - d, 2 - side],
            send_sem=y_send.at[2 * message + d],
            recv_sem=y_recv.at[2 * message + 1 - d],
            device_id=((w, left, right)[side], down if d == 0 else up),
            device_id_type=MESH,
        )

    messages = (
        (py_out, py_in, pl.ds(0, 24), 0),
        (py_out, pc_in, pl.ds(0, 16), 1),
        (py_out, pc_in, pl.ds(8, 16), 2),
        (sy_out, sy_in, pl.ds(0, 72), 0),
        (sc_out, sc_in, pl.ds(0, 56), 0),
        (ay_out, ay_in, pl.ds(0, 72), 0),
        (ac_out, ac_in, pl.ds(0, 32), 1),
        (ac_out, ac_in, pl.ds(32, 32), 2),
    )

    def each_side(action):
        @pl.when(has_down)
        def _():
            action(0)

        @pl.when(has_up)
        def _():
            action(1)

    def y_send_now(message):
        each_side(lambda d: y_copy(message, d).start())

    inner = (Y0, Y0 + CY - OV)
    outer = (Y0 - OV, Y0 + CY)

    def rows_of(ref, h, c, i, y):
        return ref.at[h, i, pl.ds(y, OV), :] if c is None else ref.at[h, c, i, pl.ds(y, OV), :]

    def pack(ref, out, start, count, comps, d, ys, base=0):
        def step(k, carry):
            for h in (0, 1):
                for j, c in enumerate(comps):
                    slot = pl.ds(base + (k * len(comps) + j) * OV, OV)
                    out[d, h, slot, :] = rows_of(ref, h, c, start + k, ys[d])[...]
            return carry

        lax.fori_loop(0, count, step, 0)

    def unpack(ref, land, start, count, comps, y, base=0, add=False):
        def step(k, carry):
            for h in (0, 1):
                for j, c in enumerate(comps):
                    slot = pl.ds(base + (k * len(comps) + j) * OV, OV)
                    cell = rows_of(ref, h, c, start + k, y)
                    cell[...] = cell[...] + land[h, slot, :] if add else land[h, slot, :]
            return carry

        lax.fori_loop(0, count, step, 0)

    pen_comps, all_comps = (None,), (0, 1, 2)

    def reduce_copy(use, s, k):
        buffer, base = (total_red, peak_red)[use], 16 * s
        slot = 48 * use + base
        return pltpu.make_async_remote_copy(
            src_ref=buffer.at[base],
            dst_ref=buffer.at[base + k],
            send_sem=r_send.at[slot + k],
            recv_sem=r_recv.at[slot + k],
            device_id=stages[s][k - 1],
            device_id_type=MESH,
        )

    def reduce_start(use, s, value):
        (total_red, peak_red)[use][16 * s] = value
        for k in range(1, len(stages[s]) + 1):
            reduce_copy(use, s, k).start()

    def reduce_finish(use, s, combine):
        for k in range(1, len(stages[s]) + 1):
            reduce_copy(use, s, k).wait_recv()
        value = [(total_red, peak_red)[use][16 * s + k] for k in range(len(stages[s]) + 1)]
        while len(value) > 1:
            value = [combine(value[2 * k], value[2 * k + 1]) for k in range(len(value) // 2)]
        return value[0]

    for copy in loads[:2]:
        copy.wait()
    each_side(lambda d: pack(pen, py_out, X0, CX, pen_comps, d, inner))
    for message in (0, 1, 2):
        y_send_now(message)
    for copy in loads[2:]:
        copy.wait()

    spot = (lax.broadcasted_iota(jnp.int32, (N, W), 0) == n) & (
        lax.broadcasted_iota(jnp.int32, (N, W), 1) == w
    )
    own_group = jnp.sum(jnp.where(spot, owner[...].astype(F32), 0.0), axis=(0, 1), keepdims=True)
    pick = (lax.broadcasted_iota(jnp.int32, (1, LANES), 1).astype(F32) == own_group).astype(F32)
    row = lax.broadcasted_iota(jnp.int32, (8, LANES), 0)
    sums = jnp.zeros((8, LANES), F32)
    for k, ref in enumerate((s_src, a_src)):
        for c in range(3):

            def add(i, total, ref=ref, c=c):
                cells = ref[0, c, i, pl.ds(Y0, CY), :] + ref[1, c, i, pl.ds(Y0, CY), :]
                return total + ((cells[0:8] + cells[8:16]) + (cells[16:24] + cells[24:32]))

            total = lax.fori_loop(X0, X0 + CX, add, jnp.zeros((8, LANES), F32))
            mean = jnp.sum(total, axis=(0, 1), keepdims=True) * (1.0 / (CX * CY * 2 * LANES))
            sums = sums + jnp.where(row == 3 * k + c, mean * pick, 0.0)
    reduce_start(0, 0, sums)

    for d, h in both:
        x_copy(STATE, d, h).start()
    each_side(lambda d: pack(s_src, sy_out, X0, CX, all_comps, d, inner))
    y_send_now(3)

    zero_margins(a_src)
    for ref in (s_a, s_b, a_a, a_b):
        zero_margins(ref)
    zero_rows(a_src, (1, 2, 3, 12, 13, 14))
    zero_rows(a_a, (0, 1, 2, 3, 12, 13, 14, 15))
    zero_rows(a_b, (1, 2, 13, 14))

    width = margin[0, 0]
    column = lax.broadcasted_iota(jnp.int32, (BOX_NY, LANES), 0) + (BOX_Y - Y0)
    place = column + n * CY
    in_y = (column >= -width) & (column < CY + width) & (place >= 0) & (place < N * CY)

    def y_arrived(message, d):
        y_copy(message, 1 - d).wait_recv()

    for d, h in both:
        x_copy(PEN, d, h).wait_recv()
    for message in (0, 1, 2):
        each_side(lambda d, message=message: y_arrived(message, d))

    def unpack_penalty(d):
        unpack(pen, py_in.at[d], X0, CX, pen_comps, outer[d])
        unpack(pen, pc_in.at[d, 0], 1, OV, pen_comps, outer[d], base=7)
        unpack(pen, pc_in.at[d, 1], 12, OV, pen_comps, outer[d])

    each_side(unpack_penalty)

    def set_gain(i, carry):
        line = jnp.zeros((BOX_NY, LANES), jnp.int32) + (i - X0)
        inside = in_y & (line >= -width) & (line < CX + width)
        for h in (0, 1):
            value = DAMPING / (8.0 + pen[h, i, pl.ds(BOX_Y, BOX_NY), :])
            gain[h, i, pl.ds(BOX_Y, BOX_NY), :] = jnp.where(inside, value, 0.0)
        return carry

    lax.fori_loop(1, XR - 1, set_gain, 0)

    reduce_start(0, 1, reduce_finish(0, 0, jnp.add))

    def adjoint_first(i, carry):
        for h in (0, 1):
            g = gain[h, i, pl.ds(Y0, CY), :]
            for c in range(3):
                a_a[h, c, i, pl.ds(Y0, CY), :] = g * a_src[h, c, i, pl.ds(Y0, CY), :]
        return carry

    lax.fori_loop(X0, X0 + CX, adjoint_first, 0)
    sweep(a_a, a_b, a_src, gain, 3, 12)
    sweep(a_b, a_a, a_src, gain, 2, 13)
    for lo, hi in ((1, 3), (12, 14)):
        sweep(a_a, a_b, a_src, gain, lo, hi)
    for d, h in both:
        adjoint_copy(d, h).start()
    each_side(lambda d: pack(a_b, ac_out, 1, OV, all_comps, d, outer))
    each_side(lambda d: pack(a_b, ac_out, 12, OV, all_comps, d, outer, base=32))
    y_send_now(6)
    y_send_now(7)
    sweep(a_a, a_b, a_src, gain, 4, 11)
    each_side(lambda d: pack(a_b, ay_out, X0, CX, all_comps, d, outer))
    y_send_now(5)

    for d, h in both:
        x_copy(STATE, d, h).wait_recv()
    each_side(lambda d: pack(s_src, sc_out, 1, OV, all_comps, d, inner))
    each_side(lambda d: pack(s_src, sc_out, 12, OV, all_comps, d, inner, base=27))
    y_send_now(4)

    each_side(lambda d: y_arrived(3, d))
    each_side(lambda d: unpack(s_src, sy_in.at[d], X0, CX, all_comps, outer[d]))
    each_side(lambda d: y_arrived(4, d))

    def unpack_corners(d):
        unpack(s_src, sc_in.at[d], 1, OV, all_comps, outer[d])
        unpack(s_src, sc_in.at[d], 12, OV, all_comps, outer[d], base=27)

    each_side(unpack_corners)

    def state_first(i, carry):
        for h in (0, 1):
            g = gain[h, i, pl.ds(BOX_Y, BOX_NY), :]
            for c in range(3):
                s_a[h, c, i, pl.ds(BOX_Y, BOX_NY), :] = g * s_src[h, c, i, pl.ds(BOX_Y, BOX_NY), :]
        return carry

    lax.fori_loop(1, XR - 1, state_first, 0)
    sweep(s_a, s_b, s_src, gain, 2, 13)
    sweep(s_b, s_a, s_src, gain, 3, 12)
    sweep(s_a, s_b, s_src, gain, 4, 11, Y0, CY)

    coarse = reduce_finish(0, 1, jnp.add)
    inv = inverse[...]
    across = lax.broadcasted_iota(jnp.int32, (GROUPS, GROUPS), 1)
    along = lax.broadcasted_iota(jnp.int32, (GROUPS, GROUPS), 0)
    rhs = coarse[:, :GROUPS]
    state_row = jnp.sum(
        ((along.astype(F32) == own_group).astype(F32) - 1.0 / GROUPS) * inv, axis=0, keepdims=True
    )
    adjoint_column = jnp.sum(
        (across.astype(F32) == own_group).astype(F32) * inv, axis=1, keepdims=True
    )
    adjoint_row = jnp.sum(jnp.where(along == across, adjoint_column, 0.0), axis=0, keepdims=True)
    centred = rhs - jnp.sum(rhs, axis=1, keepdims=True) * (1.0 / GROUPS)
    by_state = jnp.sum(rhs * state_row, axis=1, keepdims=True)
    by_adjoint = jnp.sum(centred * adjoint_row, axis=1, keepdims=True)
    corr[...] = jnp.where(row < 3, by_state, by_adjoint)

    for message in (5, 6, 7):
        each_side(lambda d, message=message: y_arrived(message, d))

    def add_from_side(d):
        unpack(a_b, ay_in.at[d], X0, CX, all_comps, inner[d], add=True)
        unpack(a_b, ac_in.at[d, 0], X0, OV, all_comps, inner[d], add=True)
        unpack(a_b, ac_in.at[d, 1], X0 + CX - OV, OV, all_comps, inner[d], add=True)

    each_side(add_from_side)
    for d, h in both:
        adjoint_copy(d, h).wait_recv()

    def add_shares(k, carry):
        for h in (0, 1):
            for c in range(3):
                for d, x in ((0, X0), (1, X0 + CX - OV)):
                    a_b[h, c, x + k, pl.ds(Y0, CY), :] = (
                        a_b[h, c, x + k, pl.ds(Y0, CY), :] + ax_in[d, h, c, k]
                    )
        return carry

    for d, h in both:
        adjoint_copy(d, h).wait_send()
    lax.fori_loop(0, OV, add_shares, 0)

    def finish(i, peak):
        for h in (0, 1):
            z = slice(h * LANES, (h + 1) * LANES)
            raw = None
            for c in range(3):
                s = s_b[h, c, X0 + i, pl.ds(Y0, CY), :] + corr[pl.ds(c, 1), :]
                a = a_b[h, c, X0 + i, pl.ds(Y0, CY), :] + corr[pl.ds(c + 3, 1), :]
                state_out[c, i, :, z] = s
                adjoint_out[c, i, :, z] = a
                raw = s * a if raw is None else raw + s * a
            sens_out[i, :, z] = -raw
            size = jnp.abs(raw)
            peak = jnp.maximum(
                peak,
                jnp.maximum(jnp.maximum(size[0:8], size[8:16]), jnp.maximum(size[16:24], size[24:32])),
            )
        return peak

    peak = lax.fori_loop(0, CX, finish, jnp.zeros((8, LANES), F32))
    peak = jnp.max(peak, axis=0, keepdims=True)
    for s in (0, 1):
        reduce_start(1, s, peak)
        peak = reduce_finish(1, s, jnp.maximum)
    scale = 1.0 / (jnp.max(peak, axis=(0, 1), keepdims=True) + PEAK_EPS)

    def normalise(i, carry):
        sens_out[i] = sens_out[i] * scale
        return carry

    lax.fori_loop(0, CX, normalise, 0)

    for which in (PEN, STATE):
        for d, h in both:
            x_copy(which, d, h).wait_send()
    for message in range(8):
        each_side(lambda d, message=message: y_copy(message, d).wait_send())
    for use in (0, 1):
        for s in (0, 1):
            for k in range(1, len(stages[s]) + 1):
                reduce_copy(use, s, k).wait_send()


def write_out(state, adjoint, sens, state_out, adjoint_out, sens_out, sem):
    copies = [
        pltpu.make_async_copy(ref, out, sem.at[k])
        for k, (ref, out) in enumerate(
            ((state, state_out), (adjoint, adjoint_out), (sens, sens_out))
        )
    ]
    for copy in copies:
        copy.start()
    for copy in copies:
        copy.wait()


def body(state_rhs, adjoint_rhs, penalty, margin_width, owner_map, coarse_inv):
    vmem = pltpu.VMEM
    field = vmem((2, 3, XR, YR, LANES), F32)
    flat = vmem((2, XR, YR, LANES), F32)

    def message(rows):
        return [vmem((2, 2, rows, LANES), F32)] * 2

    dma = pltpu.SemaphoreType.DMA
    results = pl.pallas_call(
        kernel,
        out_shape=(
            pltpu.VMEM(state_rhs.shape, F32),
            pltpu.VMEM(adjoint_rhs.shape, F32),
            pltpu.VMEM(penalty.shape, F32),
        ),
        in_specs=[pl.BlockSpec(memory_space=pl.ANY)] * 3
        + [pl.BlockSpec(memory_space=pltpu.SMEM)]
        + [pl.BlockSpec(memory_space=vmem)] * 2,
        out_specs=(pl.BlockSpec(memory_space=vmem),) * 3,
        scratch_shapes=[field] * 6
        + [flat] * 2
        + message(24)
        + [vmem((2, 2, 2, 16, LANES), F32)]
        + message(72)
        + message(56)
        + message(72)
        + [
            vmem((2, 2, 64, LANES), F32),
            vmem((2, 2, 2, 32, LANES), F32),
            vmem((2, 2, 3, OV, CY, LANES), F32),
            vmem((48, 8, LANES), F32),
            vmem((48, 1, LANES), F32),
            vmem((8, LANES), F32),
            dma((6,)),
            dma((12,)),
            dma((12,)),
            dma((16,)),
            dma((16,)),
            dma((96,)),
            dma((96,)),
        ],
        compiler_params=pltpu.CompilerParams(
            collective_id=0, has_side_effects=True, vmem_limit_bytes=56 * 1024 * 1024
        ),
        name="schwarz",
    )(
        pltpu.with_memory_space_constraint(state_rhs, pltpu.HBM),
        pltpu.with_memory_space_constraint(adjoint_rhs, pltpu.HBM),
        pltpu.with_memory_space_constraint(penalty, pltpu.HBM),
        margin_width,
        owner_map.T,
        coarse_inv,
    )
    return pl.pallas_call(
        write_out,
        out_shape=tuple(jax.ShapeDtypeStruct(r.shape, F32) for r in results),
        in_specs=[pl.BlockSpec(memory_space=vmem)] * 3,
        out_specs=(pl.BlockSpec(memory_space=pltpu.HBM),) * 3,
        scratch_shapes=[dma((3,))],
        compiler_params=pltpu.CompilerParams(vmem_limit_bytes=2 * 1024 * 1024),
        name="write_out",
    )(*results)


def solution(mesh):
    placed = (
        P(None, "wide", "narrow", None),
        P(None, "wide", "narrow", None),
        P("wide", "narrow", None),
        P("wide", "narrow"),
        P(),
        P(),
    )
    return jax.shard_map(
        body,
        mesh=mesh,
        in_specs=placed,
        out_specs=(
            P(None, "wide", "narrow", None),
            P(None, "wide", "narrow", None),
            P("wide", "narrow", None),
        ),
        check_vma=False,
    )
```

time: 91.6 us -> 80.4 us (0.88)
  Pallas kernels: 86.1 us -> 78.9 us
  local copies, waits for them, and re-layouts: 3.96 us -> 0 us
    pallas_call x1 -> x2, Pallas kernels: 86.1 us -> 78.9 us  [the longest x1 77.6 us: body(): pl.pallas_call(kernel, out_shape=(pltpu.VMEM(state_rhs.shape, F32), pltpu...]
    unnamed x7 -> x0, local copies, waits for them, and re-layouts: 3.96 us -> none
where the time goes in v2:
time: 80.4 us; the launch traced here: 80.2 us
  Pallas kernels  78.9 us (98%)
  between operations  1.29 us (2%)
    pallas_call x1, Pallas kernels, body(): pl.pallas_call(kernel, out_shape=(pltpu.VMEM(state_rhs.shape, F32), pltpu...  77.6 us

profile of v2, /device:TPU:1, one launch (start us, length us, event | category | flops | bytes accessed | tf_op | source)
XLA Modules:
  0.0 80.2 jit_solution(10141511204147116647)
XLA Ops:
  1.3 77.6 %schwarz.1 = (f32[3,8,32,256]{3,2,1,0:T(8,128)S(1)}, f32[3,8,32,256]{3,2,1,0:T(8,128)S(1)}, f32[8,32,256]{2,1,0:T(8,128)S(1)}) custom-call(f32[3,8,32,256]{3,2,1,0:T(8,128)} %state.1, f32[3,8,32,256]{3,2,1,0:T(8,128)} %adjoint.1, f32[8,32,256]{2,1,0:T(8,128)} %penalty.1, s32[1,1]{1,0:T(1,128)S(6)} %copy.9.margin, s32[4,128]{1,0:T(4,128)} %bitcast.1, ...), custom_call_target="tpu_custom_call" | custom-call | tf_op jit(solution)/shard_map/schwarz/pallas_call | solution.py:539
  78.9 1.2 %write_out.1 = (f32[3,8,32,256]{3,2,1,0:T(8,128)}, f32[3,8,32,256]{3,2,1,0:T(8,128)}, f32[8,32,256]{2,1,0:T(8,128)}) custom-call(f32[3,8,32,256]{3,2,1,0:T(8,128)S(1)} %get-tuple-element.6.state, f32[3,8,32,256]{3,2,1,0:T(8,128)S(1)} %get-tuple-element.7.adjoint, f32[8,32,256]{2,1,0:T(8,128)S(1)} %get-tuple-element.8.sens), custom_call_target="tpu_custom_call" | custom-call | tf_op jit(solution)/shard_map/write_out/pallas_call | solution.py:584

commit v3 on v2

--- a/solution.py
+++ b/solution.py
@@ -126,12 +126,17 @@
     pc_in,
     sy_out,
     sy_in,
-    sc_out,
     sc_in,
     ay_out,
     ay_in,
     ac_out,
     ac_in,
+    pr_out,
+    pr_in,
+    sr_out,
+    sr_in,
+    ar_out,
+    ar_in,
     ax_in,
     total_red,
     peak_red,
@@ -222,7 +227,7 @@
         x_copy(PEN, d, h).start()
 
     def y_copy(message, d):
-        out, land, rows, side = messages[message]
+        out, land, rows, side, _ = messages[message]
         return pltpu.make_async_remote_copy(
             src_ref=out.at[d, :, rows, :],
             dst_ref=land.at[1 - d, :, rows, :] if side == 0 else land.at[1 - d, 2 - side],
@@ -233,14 +238,18 @@
         )
 
     messages = (
-        (py_out, py_in, pl.ds(0, 24), 0),
-        (py_out, pc_in, pl.ds(0, 16), 1),
-        (py_out, pc_in, pl.ds(8, 16), 2),
-        (sy_out, sy_in, pl.ds(0, 72), 0),
-        (sc_out, sc_in, pl.ds(0, 56), 0),
-        (ay_out, ay_in, pl.ds(0, 72), 0),
-        (ac_out, ac_in, pl.ds(0, 32), 1),
-        (ac_out, ac_in, pl.ds(32, 32), 2),
+        (py_out, py_in, pl.ds(0, 24), 0, 0),
+        (py_out, pc_in, pl.ds(0, 16), 1, 1),
+        (py_out, pc_in, pl.ds(8, 16), 2, 1),
+        (sy_out, sy_in, pl.ds(0, 72), 0, 0),
+        (sy_out, sc_in, pl.ds(0, 32), 1, 1),
+        (sy_out, sc_in, pl.ds(40, 32), 2, 1),
+        (ay_out, ay_in, pl.ds(0, 72), 0, 0),
+        (ac_out, ac_in, pl.ds(0, 32), 1, 1),
+        (ac_out, ac_in, pl.ds(32, 32), 2, 1),
+        (pr_out, pr_in, pl.ds(0, 24), 0, 2),
+        (sr_out, sr_in, pl.ds(0, 56), 0, 2),
+        (ar_out, ar_in, pl.ds(0, 56), 0, 2),
     )
 
     def each_side(action):
@@ -252,8 +261,29 @@
         def _():
             action(1)
 
+    def off_chip(action):
+        @pl.when(n == 2)
+        def _():
+            action(0)
+
+        @pl.when(n == 1)
+        def _():
+            action(1)
+
+    def on_chip(action):
+        @pl.when(pc == 1)
+        def _():
+            action(0)
+
+        @pl.when(pc == 0)
+        def _():
+            action(1)
+
+    def sides(message):
+        return {0: each_side, 1: off_chip, 2: on_chip}[messages[message][4]]
+
     def y_send_now(message):
-        each_side(lambda d: y_copy(message, d).start())
+        sides(message)(lambda d: y_copy(message, d).start())
 
     inner = (Y0, Y0 + CY - OV)
     outer = (Y0 - OV, Y0 + CY)
@@ -336,10 +366,11 @@
             sums = sums + jnp.where(row == 3 * k + c, mean * pick, 0.0)
     reduce_start(0, 0, sums)
 
+    each_side(lambda d: pack(s_src, sy_out, X0, CX, all_comps, d, inner))
+    for message in (3, 4, 5):
+        y_send_now(message)
     for d, h in both:
         x_copy(STATE, d, h).start()
-    each_side(lambda d: pack(s_src, sy_out, X0, CX, all_comps, d, inner))
-    y_send_now(3)
 
     zero_margins(a_src)
     for ref in (s_a, s_b, a_a, a_b):
@@ -358,15 +389,25 @@
 
     for d, h in both:
         x_copy(PEN, d, h).wait_recv()
+    on_chip(lambda d: pack(pen, pr_out, 1, OV, pen_comps, d, inner))
+    on_chip(lambda d: pack(pen, pr_out, 12, OV, pen_comps, d, inner, base=9))
+    y_send_now(9)
     for message in (0, 1, 2):
-        each_side(lambda d, message=message: y_arrived(message, d))
+        sides(message)(lambda d, message=message: y_arrived(message, d))
+    each_side(lambda d: unpack(pen, py_in.at[d], X0, CX, pen_comps, outer[d]))
 
     def unpack_penalty(d):
-        unpack(pen, py_in.at[d], X0, CX, pen_comps, outer[d])
         unpack(pen, pc_in.at[d, 0], 1, OV, pen_comps, outer[d], base=7)
         unpack(pen, pc_in.at[d, 1], 12, OV, pen_comps, outer[d])
 
-    each_side(unpack_penalty)
+    off_chip(unpack_penalty)
+
+    def unpack_relayed_penalty(d):
+        y_arrived(9, d)
+        unpack(pen, pr_in.at[d], 1, OV, pen_comps, outer[d])
+        unpack(pen, pr_in.at[d], 12, OV, pen_comps, outer[d], base=9)
+
+    on_chip(unpack_relayed_penalty)
 
     def set_gain(i, carry):
         line = jnp.zeros((BOX_NY, LANES), jnp.int32) + (i - X0)
@@ -390,33 +431,45 @@
     lax.fori_loop(X0, X0 + CX, adjoint_first, 0)
     sweep(a_a, a_b, a_src, gain, 3, 12)
     sweep(a_b, a_a, a_src, gain, 2, 13)
-    for lo, hi in ((1, 3), (12, 14)):
-        sweep(a_a, a_b, a_src, gain, lo, hi)
+    sweep(a_a, a_b, a_src, gain, 1, 14)
+    each_side(lambda d: pack(a_b, ay_out, X0, CX, all_comps, d, outer))
+    off_chip(lambda d: pack(a_b, ac_out, 1, OV, all_comps, d, outer))
+    off_chip(lambda d: pack(a_b, ac_out, 12, OV, all_comps, d, outer, base=32))
+    on_chip(lambda d: pack(a_b, ar_out, 1, OV, all_comps, d, outer))
+    on_chip(lambda d: pack(a_b, ar_out, 12, OV, all_comps, d, outer, base=27))
+    for message in (11, 6, 7, 8):
+        y_send_now(message)
+
+    def add_relayed(d):
+        y_arrived(11, d)
+        unpack(a_b, ar_in.at[d], 1, OV, all_comps, inner[d], add=True)
+        unpack(a_b, ar_in.at[d], 12, OV, all_comps, inner[d], base=27, add=True)
+
+    on_chip(add_relayed)
     for d, h in both:
         adjoint_copy(d, h).start()
-    each_side(lambda d: pack(a_b, ac_out, 1, OV, all_comps, d, outer))
-    each_side(lambda d: pack(a_b, ac_out, 12, OV, all_comps, d, outer, base=32))
-    y_send_now(6)
-    y_send_now(7)
-    sweep(a_a, a_b, a_src, gain, 4, 11)
-    each_side(lambda d: pack(a_b, ay_out, X0, CX, all_comps, d, outer))
-    y_send_now(5)
 
     for d, h in both:
         x_copy(STATE, d, h).wait_recv()
-    each_side(lambda d: pack(s_src, sc_out, 1, OV, all_comps, d, inner))
-    each_side(lambda d: pack(s_src, sc_out, 12, OV, all_comps, d, inner, base=27))
-    y_send_now(4)
-
-    each_side(lambda d: y_arrived(3, d))
+    on_chip(lambda d: pack(s_src, sr_out, 1, OV, all_comps, d, inner))
+    on_chip(lambda d: pack(s_src, sr_out, 12, OV, all_comps, d, inner, base=27))
+    y_send_now(10)
+    for message in (3, 4, 5):
+        sides(message)(lambda d, message=message: y_arrived(message, d))
     each_side(lambda d: unpack(s_src, sy_in.at[d], X0, CX, all_comps, outer[d]))
-    each_side(lambda d: y_arrived(4, d))
-
-    def unpack_corners(d):
-        unpack(s_src, sc_in.at[d], 1, OV, all_comps, outer[d])
-        unpack(s_src, sc_in.at[d], 12, OV, all_comps, outer[d], base=27)
-
-    each_side(unpack_corners)
+
+    def unpack_state(d):
+        unpack(s_src, sc_in.at[d, 0], 1, OV, all_comps, outer[d], base=5)
+        unpack(s_src, sc_in.at[d, 1], 12, OV, all_comps, outer[d])
+
+    off_chip(unpack_state)
+
+    def unpack_relayed_state(d):
+        y_arrived(10, d)
+        unpack(s_src, sr_in.at[d], 1, OV, all_comps, outer[d])
+        unpack(s_src, sr_in.at[d], 12, OV, all_comps, outer[d], base=27)
+
+    on_chip(unpack_relayed_state)
 
     def state_first(i, carry):
         for h in (0, 1):
@@ -447,15 +500,15 @@
     by_adjoint = jnp.sum(centred * adjoint_row, axis=1, keepdims=True)
     corr[...] = jnp.where(row < 3, by_state, by_adjoint)
 
-    for message in (5, 6, 7):
-        each_side(lambda d, message=message: y_arrived(message, d))
+    for message in (6, 7, 8):
+        sides(message)(lambda d, message=message: y_arrived(message, d))
+    each_side(lambda d: unpack(a_b, ay_in.at[d], X0, CX, all_comps, inner[d], add=True))
 
     def add_from_side(d):
-        unpack(a_b, ay_in.at[d], X0, CX, all_comps, inner[d], add=True)
         unpack(a_b, ac_in.at[d, 0], X0, OV, all_comps, inner[d], add=True)
         unpack(a_b, ac_in.at[d, 1], X0 + CX - OV, OV, all_comps, inner[d], add=True)
 
-    each_side(add_from_side)
+    off_chip(add_from_side)
     for d, h in both:
         adjoint_copy(d, h).wait_recv()
 
@@ -506,8 +559,8 @@
     for which in (PEN, STATE):
         for d, h in both:
             x_copy(which, d, h).wait_send()
-    for message in range(8):
-        each_side(lambda d, message=message: y_copy(message, d).wait_send())
+    for message in range(len(messages)):
+        sides(message)(lambda d, message=message: y_copy(message, d).wait_send())
     for use in (0, 1):
         for s in (0, 1):
             for k in range(1, len(stages[s]) + 1):
@@ -552,11 +605,16 @@
         + message(24)
         + [vmem((2, 2, 2, 16, LANES), F32)]
         + message(72)
-        + message(56)
+        + [vmem((2, 2, 2, 32, LANES), F32)]
         + message(72)
         + [
             vmem((2, 2, 64, LANES), F32),
             vmem((2, 2, 2, 32, LANES), F32),
+        ]
+        + message(24)
+        + message(56)
+        + message(56)
+        + [
             vmem((2, 2, 3, OV, CY, LANES), F32),
             vmem((48, 8, LANES), F32),
             vmem((48, 1, LANES), F32),
@@ -564,8 +622,8 @@
             dma((6,)),
             dma((12,)),
             dma((12,)),
-            dma((16,)),
-            dma((16,)),
+            dma((24,)),
+            dma((24,)),
             dma((96,)),
             dma((96,)),
         ],

time: 80.4 us -> 73 us (0.908)
  Pallas kernels: 78.9 us -> 71.5 us
    pallas_call x1, Pallas kernels: 77.6 us -> 70.2 us  [body(): pl.pallas_call(kernel, out_shape=(pltpu.VMEM(state_rhs.shape, F32), pltpu...]
where the time goes in v3:
time: 73 us; the launch traced here: 72.8 us
  Pallas kernels  71.5 us (98%)
  between operations  1.29 us (2%)
    pallas_call x1, Pallas kernels, body(): pl.pallas_call(kernel, out_shape=(pltpu.VMEM(state_rhs.shape, F32), pltpu...  70.2 us

profile of v3, /device:TPU:1, one launch (start us, length us, event | category | flops | bytes accessed | tf_op | source)
XLA Modules:
  0.0 72.8 jit_solution(16074585428558801677)
XLA Ops:
  1.3 70.2 %schwarz.1 = (f32[3,8,32,256]{3,2,1,0:T(8,128)S(1)}, f32[3,8,32,256]{3,2,1,0:T(8,128)S(1)}, f32[8,32,256]{2,1,0:T(8,128)S(1)}) custom-call(f32[3,8,32,256]{3,2,1,0:T(8,128)} %state.1, f32[3,8,32,256]{3,2,1,0:T(8,128)} %adjoint.1, f32[8,32,256]{2,1,0:T(8,128)} %penalty.1, s32[1,1]{1,0:T(1,128)S(6)} %copy.9.margin, s32[4,128]{1,0:T(4,128)} %bitcast.1, ...), custom_call_target="tpu_custom_call" | custom-call | tf_op jit(solution)/shard_map/schwarz/pallas_call | solution.py:592
  71.5 1.2 %write_out.1 = (f32[3,8,32,256]{3,2,1,0:T(8,128)}, f32[3,8,32,256]{3,2,1,0:T(8,128)}, f32[8,32,256]{2,1,0:T(8,128)}) custom-call(f32[3,8,32,256]{3,2,1,0:T(8,128)S(1)} %get-tuple-element.6.state, f32[3,8,32,256]{3,2,1,0:T(8,128)S(1)} %get-tuple-element.7.adjoint, f32[8,32,256]{2,1,0:T(8,128)S(1)} %get-tuple-element.8.sens), custom_call_target="tpu_custom_call" | custom-call | tf_op jit(solution)/shard_map/write_out/pallas_call | solution.py:642

commit v4 on v3

--- a/solution.py
+++ b/solution.py
@@ -316,13 +316,24 @@
 
     def reduce_copy(use, s, k):
         buffer, base = (total_red, peak_red)[use], 16 * s
-        slot = 48 * use + base
         return pltpu.make_async_remote_copy(
             src_ref=buffer.at[base],
             dst_ref=buffer.at[base + k],
-            send_sem=r_send.at[slot + k],
-            recv_sem=r_recv.at[slot + k],
+            send_sem=r_send.at[2 * use + s],
+            recv_sem=r_recv.at[2 * use + s],
             device_id=stages[s][k - 1],
+            device_id_type=MESH,
+        )
+
+    def reduce_all(use, s):
+        count = len(stages[s])
+        slots = (total_red, peak_red)[use].at[pl.ds(16 * s + 1, count)]
+        return pltpu.make_async_remote_copy(
+            src_ref=slots,
+            dst_ref=slots,
+            send_sem=r_send.at[2 * use + s],
+            recv_sem=r_recv.at[2 * use + s],
+            device_id=stages[s][0],
             device_id_type=MESH,
         )
 
@@ -332,8 +343,7 @@
             reduce_copy(use, s, k).start()
 
     def reduce_finish(use, s, combine):
-        for k in range(1, len(stages[s]) + 1):
-            reduce_copy(use, s, k).wait_recv()
+        reduce_all(use, s).wait_recv()
         value = [(total_red, peak_red)[use][16 * s + k] for k in range(len(stages[s]) + 1)]
         while len(value) > 1:
             value = [combine(value[2 * k], value[2 * k + 1]) for k in range(len(value) // 2)]
@@ -418,8 +428,6 @@
         return carry
 
     lax.fori_loop(1, XR - 1, set_gain, 0)
-
-    reduce_start(0, 1, reduce_finish(0, 0, jnp.add))
 
     def adjoint_first(i, carry):
         for h in (0, 1):
@@ -449,6 +457,8 @@
     for d, h in both:
         adjoint_copy(d, h).start()
 
+    reduce_start(0, 1, reduce_finish(0, 0, jnp.add))
+
     for d, h in both:
         x_copy(STATE, d, h).wait_recv()
     on_chip(lambda d: pack(s_src, sr_out, 1, OV, all_comps, d, inner))
@@ -509,31 +519,27 @@
         unpack(a_b, ac_in.at[d, 1], X0 + CX - OV, OV, all_comps, inner[d], add=True)
 
     off_chip(add_from_side)
-    for d, h in both:
-        adjoint_copy(d, h).wait_recv()
-
-    def add_shares(k, carry):
-        for h in (0, 1):
+
+    def correct(i, carry):
+        for h in (0, 1):
+            z = slice(h * LANES, (h + 1) * LANES)
             for c in range(3):
-                for d, x in ((0, X0), (1, X0 + CX - OV)):
-                    a_b[h, c, x + k, pl.ds(Y0, CY), :] = (
-                        a_b[h, c, x + k, pl.ds(Y0, CY), :] + ax_in[d, h, c, k]
-                    )
+                state_out[c, i, :, z] = s_b[h, c, X0 + i, pl.ds(Y0, CY), :] + corr[pl.ds(c, 1), :]
+                adjoint_out[c, i, :, z] = a_b[h, c, X0 + i, pl.ds(Y0, CY), :] + corr[pl.ds(c + 3, 1), :]
         return carry
 
-    for d, h in both:
-        adjoint_copy(d, h).wait_send()
-    lax.fori_loop(0, OV, add_shares, 0)
-
-    def finish(i, peak):
+    lax.fori_loop(0, CX, correct, 0)
+
+    def product(i, peak, share=None):
         for h in (0, 1):
             z = slice(h * LANES, (h + 1) * LANES)
             raw = None
             for c in range(3):
-                s = s_b[h, c, X0 + i, pl.ds(Y0, CY), :] + corr[pl.ds(c, 1), :]
-                a = a_b[h, c, X0 + i, pl.ds(Y0, CY), :] + corr[pl.ds(c + 3, 1), :]
-                state_out[c, i, :, z] = s
-                adjoint_out[c, i, :, z] = a
+                a = adjoint_out[c, i, :, z]
+                if share is not None:
+                    a = a + share[h, c]
+                    adjoint_out[c, i, :, z] = a
+                s = state_out[c, i, :, z]
                 raw = s * a if raw is None else raw + s * a
             sens_out[i, :, z] = -raw
             size = jnp.abs(raw)
@@ -543,28 +549,40 @@
             )
         return peak
 
-    peak = lax.fori_loop(0, CX, finish, jnp.zeros((8, LANES), F32))
-    peak = jnp.max(peak, axis=0, keepdims=True)
+    peak = lax.fori_loop(OV, CX - OV, product, jnp.zeros((8, LANES), F32))
+    for d, base in ((0, 0), (1, CX - OV)):
+        for h in (0, 1):
+            adjoint_copy(1 - d, h).wait_recv()
+
+        def with_share(k, peak, d=d, base=base):
+            share = {(h, c): ax_in[d, h, c, k] for h in (0, 1) for c in range(3)}
+            return product(base + k, peak, share)
+
+        peak = lax.fori_loop(0, OV, with_share, peak)
+
+    reduce_start(1, 0, jnp.max(peak, axis=0, keepdims=True))
+
+    for which in (PEN, STATE):
+        for d, h in both:
+            x_copy(which, d, h).wait_send()
+    for d, h in both:
+        adjoint_copy(d, h).wait_send()
+    for message in range(len(messages)):
+        sides(message)(lambda d, message=message: y_copy(message, d).wait_send())
     for s in (0, 1):
-        reduce_start(1, s, peak)
-        peak = reduce_finish(1, s, jnp.maximum)
-    scale = 1.0 / (jnp.max(peak, axis=(0, 1), keepdims=True) + PEAK_EPS)
+        reduce_all(0, s).wait_send()
+
+    reduce_start(1, 1, reduce_finish(1, 0, jnp.maximum))
+    reduce_all(1, 0).wait_send()
+    peak = reduce_finish(1, 1, jnp.maximum)
+    scale = 1.0 / (jnp.max(peak, axis=1, keepdims=True) + PEAK_EPS)
 
     def normalise(i, carry):
         sens_out[i] = sens_out[i] * scale
         return carry
 
     lax.fori_loop(0, CX, normalise, 0)
-
-    for which in (PEN, STATE):
-        for d, h in both:
-            x_copy(which, d, h).wait_send()
-    for message in range(len(messages)):
-        sides(message)(lambda d, message=message: y_copy(message, d).wait_send())
-    for use in (0, 1):
-        for s in (0, 1):
-            for k in range(1, len(stages[s]) + 1):
-                reduce_copy(use, s, k).wait_send()
+    reduce_all(1, 1).wait_send()
 
 
 def write_out(state, adjoint, sens, state_out, adjoint_out, sens_out, sem):
@@ -624,8 +642,8 @@
             dma((12,)),
             dma((24,)),
             dma((24,)),
-            dma((96,)),
-            dma((96,)),
+            dma((4,)),
+            dma((4,)),
         ],
         compiler_params=pltpu.CompilerParams(
             collective_id=0, has_side_effects=True, vmem_limit_bytes=56 * 1024 * 1024

time: 73 us -> 68.6 us (0.940)
  Pallas kernels: 71.5 us -> 67.1 us
    pallas_call x1, Pallas kernels: 70.2 us -> 65.9 us  [body(): pl.pallas_call(kernel, out_shape=(pltpu.VMEM(state_rhs.shape, F32), pltpu...]
where the time goes in v4:
time: 68.6 us; the launch traced here: 68.4 us
  Pallas kernels  67.1 us (98%)
  between operations  1.29 us (2%)
    pallas_call x1, Pallas kernels, body(): pl.pallas_call(kernel, out_shape=(pltpu.VMEM(state_rhs.shape, F32), pltpu...  65.9 us

profile of v4, /device:TPU:1, one launch (start us, length us, event | category | flops | bytes accessed | tf_op | source)
XLA Modules:
  0.0 68.4 jit_solution(7361514379396125488)
XLA Ops:
  1.3 65.9 %schwarz.1 = (f32[3,8,32,256]{3,2,1,0:T(8,128)S(1)}, f32[3,8,32,256]{3,2,1,0:T(8,128)S(1)}, f32[8,32,256]{2,1,0:T(8,128)S(1)}) custom-call(f32[3,8,32,256]{3,2,1,0:T(8,128)} %state.1, f32[3,8,32,256]{3,2,1,0:T(8,128)} %adjoint.1, f32[8,32,256]{2,1,0:T(8,128)} %penalty.1, s32[1,1]{1,0:T(1,128)S(6)} %copy.9.margin, s32[4,128]{1,0:T(4,128)} %bitcast.1, ...), custom_call_target="tpu_custom_call" | custom-call | tf_op jit(solution)/shard_map/schwarz/pallas_call | solution.py:610
  67.2 1.2 %write_out.1 = (f32[3,8,32,256]{3,2,1,0:T(8,128)}, f32[3,8,32,256]{3,2,1,0:T(8,128)}, f32[8,32,256]{2,1,0:T(8,128)}) custom-call(f32[3,8,32,256]{3,2,1,0:T(8,128)S(1)} %get-tuple-element.6.state, f32[3,8,32,256]{3,2,1,0:T(8,128)S(1)} %get-tuple-element.7.adjoint, f32[8,32,256]{2,1,0:T(8,128)S(1)} %get-tuple-element.8.sens), custom_call_target="tpu_custom_call" | custom-call | tf_op jit(solution)/shard_map/write_out/pallas_call | solution.py:660

commit v5 on v4

--- a/solution.py
+++ b/solution.py
@@ -26,7 +26,7 @@
 Y0 = 8
 BOX_Y = 5
 BOX_NY = 40
-PEN, STATE = 0, 1
+PEN, STATE, FIRST = 0, 1, 2
 
 
 def next_and_previous(plus, minus, lane):
@@ -138,6 +138,7 @@
     ar_out,
     ar_in,
     ax_in,
+    first_out,
     total_red,
     peak_red,
     corr,
@@ -196,17 +197,21 @@
     pl.semaphore_wait(barrier, peers)
 
     def x_copy(which, d, h):
-        rows, target = (pl.ds(0, OV), pl.ds(12, OV)) if d == 0 else (pl.ds(CX - OV, OV), pl.ds(1, OV))
         z, own_y = pl.ds(h * LANES, LANES), pl.ds(Y0, CY)
-        if which == PEN:
-            ref, to = penalty.at[rows, :, z], pen.at[h, target, own_y, :]
+        if which == FIRST:
+            ref, to = first_out.at[d, h], s_src.at[h, :, 14 if d == 0 else 1, own_y, :]
         else:
-            ref, to = state.at[:, rows, :, z], s_src.at[h, :, target, own_y, :]
+            rows, target = (pl.ds(0, 2), pl.ds(12, 2)) if d == 0 else (pl.ds(CX - 2, 2), pl.ds(2, 2))
+            if which == PEN:
+                ref, to = penalty.at[rows, :, z], pen.at[h, target, own_y, :]
+            else:
+                ref, to = state.at[:, rows, :, z], s_src.at[h, :, target, own_y, :]
+        slot = 4 * which if which < FIRST else 12
         return pltpu.make_async_remote_copy(
             src_ref=ref,
             dst_ref=to,
-            send_sem=x_send.at[4 * which + 2 * d + h],
-            recv_sem=x_recv.at[4 * which + 2 * (1 - d) + h],
+            send_sem=x_send.at[slot + 2 * d + h],
+            recv_sem=x_recv.at[slot + 2 * (1 - d) + h],
             device_id=(left if d == 0 else right, n),
             device_id_type=MESH,
         )
@@ -247,7 +252,7 @@
         (ay_out, ay_in, pl.ds(0, 72), 0, 0),
         (ac_out, ac_in, pl.ds(0, 32), 1, 1),
         (ac_out, ac_in, pl.ds(32, 32), 2, 1),
-        (pr_out, pr_in, pl.ds(0, 24), 0, 2),
+        (pr_out, pr_in, pl.ds(0, 16), 0, 2),
         (sr_out, sr_in, pl.ds(0, 56), 0, 2),
         (ar_out, ar_in, pl.ds(0, 56), 0, 2),
     )
@@ -381,6 +386,13 @@
         y_send_now(message)
     for d, h in both:
         x_copy(STATE, d, h).start()
+    for d, x in ((0, X0 + 2), (1, X0 + CX - OV)):
+        for h in (0, 1):
+            g = DAMPING / (8.0 + pen[h, x, pl.ds(Y0, CY), :])
+            for c in range(3):
+                first_out[d, h, c] = g * s_src[h, c, x, pl.ds(Y0, CY), :]
+    for d, h in both:
+        x_copy(FIRST, d, h).start()
 
     zero_margins(a_src)
     for ref in (s_a, s_b, a_a, a_b):
@@ -399,8 +411,8 @@
 
     for d, h in both:
         x_copy(PEN, d, h).wait_recv()
-    on_chip(lambda d: pack(pen, pr_out, 1, OV, pen_comps, d, inner))
-    on_chip(lambda d: pack(pen, pr_out, 12, OV, pen_comps, d, inner, base=9))
+    on_chip(lambda d: pack(pen, pr_out, 2, 2, pen_comps, d, inner))
+    on_chip(lambda d: pack(pen, pr_out, 12, 2, pen_comps, d, inner, base=6))
     y_send_now(9)
     for message in (0, 1, 2):
         sides(message)(lambda d, message=message: y_arrived(message, d))
@@ -414,20 +426,26 @@
 
     def unpack_relayed_penalty(d):
         y_arrived(9, d)
-        unpack(pen, pr_in.at[d], 1, OV, pen_comps, outer[d])
-        unpack(pen, pr_in.at[d], 12, OV, pen_comps, outer[d], base=9)
+        unpack(pen, pr_in.at[d], 2, 2, pen_comps, outer[d])
+        unpack(pen, pr_in.at[d], 12, 2, pen_comps, outer[d], base=6)
 
     on_chip(unpack_relayed_penalty)
 
-    def set_gain(i, carry):
+    def set_gain(i, carry, outermost=False):
         line = jnp.zeros((BOX_NY, LANES), jnp.int32) + (i - X0)
         inside = in_y & (line >= -width) & (line < CX + width)
         for h in (0, 1):
             value = DAMPING / (8.0 + pen[h, i, pl.ds(BOX_Y, BOX_NY), :])
+            if outermost:
+                value = jnp.where(far, value, 1.0)
             gain[h, i, pl.ds(BOX_Y, BOX_NY), :] = jnp.where(inside, value, 0.0)
         return carry
 
-    lax.fori_loop(1, XR - 1, set_gain, 0)
+    spot_y = jnp.zeros((BOX_NY, LANES), jnp.int32) + n
+    far = ((spot_y == 1) & (column >= CY)) | ((spot_y == 2) & (column < 0))
+    lax.fori_loop(2, XR - 2, set_gain, 0)
+    set_gain(1, 0, True)
+    set_gain(XR - 2, 0, True)
 
     def adjoint_first(i, carry):
         for h in (0, 1):
@@ -461,6 +479,7 @@
 
     for d, h in both:
         x_copy(STATE, d, h).wait_recv()
+        x_copy(FIRST, d, h).wait_recv()
     on_chip(lambda d: pack(s_src, sr_out, 1, OV, all_comps, d, inner))
     on_chip(lambda d: pack(s_src, sr_out, 12, OV, all_comps, d, inner, base=27))
     y_send_now(10)
@@ -550,7 +569,7 @@
         return peak
 
     peak = lax.fori_loop(OV, CX - OV, product, jnp.zeros((8, LANES), F32))
-    for d, base in ((0, 0), (1, CX - OV)):
+    for d, base, outermost in ((0, 0, 2), (1, CX - OV, 0)):
         for h in (0, 1):
             adjoint_copy(1 - d, h).wait_recv()
 
@@ -558,11 +577,14 @@
             share = {(h, c): ax_in[d, h, c, k] for h in (0, 1) for c in range(3)}
             return product(base + k, peak, share)
 
-        peak = lax.fori_loop(0, OV, with_share, peak)
+        peak = lax.fori_loop(1 - outermost // 2, OV - outermost // 2, with_share, peak)
+        g = [gain[h, X0 + base + outermost, pl.ds(Y0, CY), :] for h in (0, 1)]
+        share = {(h, c): g[h] * ax_in[d, h, c, outermost] for h in (0, 1) for c in range(3)}
+        peak = product(base + outermost, peak, share)
 
     reduce_start(1, 0, jnp.max(peak, axis=0, keepdims=True))
 
-    for which in (PEN, STATE):
+    for which in (PEN, STATE, FIRST):
         for d, h in both:
             x_copy(which, d, h).wait_send()
     for d, h in both:
@@ -629,17 +651,18 @@
             vmem((2, 2, 64, LANES), F32),
             vmem((2, 2, 2, 32, LANES), F32),
         ]
-        + message(24)
+        + message(16)
         + message(56)
         + message(56)
         + [
             vmem((2, 2, 3, OV, CY, LANES), F32),
+            vmem((2, 2, 3, CY, LANES), F32),
             vmem((48, 8, LANES), F32),
             vmem((48, 1, LANES), F32),
             vmem((8, LANES), F32),
             dma((6,)),
-            dma((12,)),
-            dma((12,)),
+            dma((16,)),
+            dma((16,)),
             dma((24,)),
             dma((24,)),
             dma((4,)),

time: 68.6 us -> 67.3 us (0.981)
  Pallas kernels: 67.1 us -> 65.8 us
    pallas_call x1, Pallas kernels: 65.9 us -> 64.5 us  [body(): pl.pallas_call(kernel, out_shape=(pltpu.VMEM(state_rhs.shape, F32), pltpu...]
where the time goes in v5:
time: 67.3 us; the launch traced here: 67.1 us
  Pallas kernels  65.8 us (98%)
  between operations  1.29 us (2%)
    pallas_call x1, Pallas kernels, body(): pl.pallas_call(kernel, out_shape=(pltpu.VMEM(state_rhs.shape, F32), pltpu...  64.5 us

profile of v5, /device:TPU:1, one launch (start us, length us, event | category | flops | bytes accessed | tf_op | source)
XLA Modules:
  0.0 67.1 jit_solution(286393592257659802)
XLA Ops:
  1.3 64.5 %schwarz.1 = (f32[3,8,32,256]{3,2,1,0:T(8,128)S(1)}, f32[3,8,32,256]{3,2,1,0:T(8,128)S(1)}, f32[8,32,256]{2,1,0:T(8,128)S(1)}) custom-call(f32[3,8,32,256]{3,2,1,0:T(8,128)} %state.1, f32[3,8,32,256]{3,2,1,0:T(8,128)} %adjoint.1, f32[8,32,256]{2,1,0:T(8,128)} %penalty.1, s32[1,1]{1,0:T(1,128)S(6)} %copy.9.margin, s32[4,128]{1,0:T(4,128)} %bitcast.1, ...), custom_call_target="tpu_custom_call" | custom-call | tf_op jit(solution)/shard_map/schwarz/pallas_call | solution.py:632
  65.8 1.2 %write_out.1 = (f32[3,8,32,256]{3,2,1,0:T(8,128)}, f32[3,8,32,256]{3,2,1,0:T(8,128)}, f32[8,32,256]{2,1,0:T(8,128)}) custom-call(f32[3,8,32,256]{3,2,1,0:T(8,128)S(1)} %get-tuple-element.6.state, f32[3,8,32,256]{3,2,1,0:T(8,128)S(1)} %get-tuple-element.7.adjoint, f32[8,32,256]{2,1,0:T(8,128)S(1)} %get-tuple-element.8.sens), custom_call_target="tpu_custom_call" | custom-call | tf_op jit(solution)/shard_map/write_out/pallas_call | solution.py:683

commit v6 on v5

--- a/solution.py
+++ b/solution.py
@@ -401,6 +401,15 @@
     zero_rows(a_a, (0, 1, 2, 3, 12, 13, 14, 15))
     zero_rows(a_b, (1, 2, 13, 14))
 
+    def adjoint_first(i, carry):
+        for h in (0, 1):
+            g = DAMPING / (8.0 + pen[h, i, pl.ds(Y0, CY), :])
+            for c in range(3):
+                a_a[h, c, i, pl.ds(Y0, CY), :] = g * a_src[h, c, i, pl.ds(Y0, CY), :]
+        return carry
+
+    lax.fori_loop(X0, X0 + CX, adjoint_first, 0)
+
     width = margin[0, 0]
     column = lax.broadcasted_iota(jnp.int32, (BOX_NY, LANES), 0) + (BOX_Y - Y0)
     place = column + n * CY
@@ -447,14 +456,6 @@
     set_gain(1, 0, True)
     set_gain(XR - 2, 0, True)
 
-    def adjoint_first(i, carry):
-        for h in (0, 1):
-            g = gain[h, i, pl.ds(Y0, CY), :]
-            for c in range(3):
-                a_a[h, c, i, pl.ds(Y0, CY), :] = g * a_src[h, c, i, pl.ds(Y0, CY), :]
-        return carry
-
-    lax.fori_loop(X0, X0 + CX, adjoint_first, 0)
     sweep(a_a, a_b, a_src, gain, 3, 12)
     sweep(a_b, a_a, a_src, gain, 2, 13)
     sweep(a_a, a_b, a_src, gain, 1, 14)

time: 67.3 us -> 67.3 us (level)
  no operation moved by 1% of the time
where the time goes in v6:
time: 67.3 us; the launch traced here: 67.1 us
  Pallas kernels  65.8 us (98%)
  between operations  1.29 us (2%)
    pallas_call x1, Pallas kernels, body(): pl.pallas_call(kernel, out_shape=(pltpu.VMEM(state_rhs.shape, F32), pltpu...  64.5 us

profile of v6, /device:TPU:1, one launch (start us, length us, event | category | flops | bytes accessed | tf_op | source)
XLA Modules:
  0.0 67.1 jit_solution(10303533075196141864)
XLA Ops:
  1.3 64.5 %schwarz.1 = (f32[3,8,32,256]{3,2,1,0:T(8,128)S(1)}, f32[3,8,32,256]{3,2,1,0:T(8,128)S(1)}, f32[8,32,256]{2,1,0:T(8,128)S(1)}) custom-call(f32[3,8,32,256]{3,2,1,0:T(8,128)} %state.1, f32[3,8,32,256]{3,2,1,0:T(8,128)} %adjoint.1, f32[8,32,256]{2,1,0:T(8,128)} %penalty.1, s32[1,1]{1,0:T(1,128)S(6)} %copy.9.margin, s32[4,128]{1,0:T(4,128)} %bitcast.1, ...), custom_call_target="tpu_custom_call" | custom-call | tf_op jit(solution)/shard_map/schwarz/pallas_call | solution.py:633
  65.8 1.2 %write_out.1 = (f32[3,8,32,256]{3,2,1,0:T(8,128)}, f32[3,8,32,256]{3,2,1,0:T(8,128)}, f32[8,32,256]{2,1,0:T(8,128)}) custom-call(f32[3,8,32,256]{3,2,1,0:T(8,128)S(1)} %get-tuple-element.6.state, f32[3,8,32,256]{3,2,1,0:T(8,128)S(1)} %get-tuple-element.7.adjoint, f32[8,32,256]{2,1,0:T(8,128)S(1)} %get-tuple-element.8.sens), custom_call_target="tpu_custom_call" | custom-call | tf_op jit(solution)/shard_map/write_out/pallas_call | solution.py:684
